TPU v7x, 32 devices: a whole 2x2x4 slice. The times are simulated.
32 devices in a mesh: groups: 2 (over y), ctx: 16 (over z, x, core).
Axes of the slice: x: 2, y: 2, z: 4, core: 2. Of those that a mesh axis runs over, the one named last changes fastest.
Arguments:
- queries: bfloat16 [12288, 1024], P(('groups', 'ctx')), parts along dimension 0, may hold values from -6 to 6
- keys: bfloat16 [12288, 1024], P(('groups', 'ctx')), parts along dimension 0, may hold values from -6 to 6
- values: bfloat16 [12288, 1024], P(('groups', 'ctx')), parts along dimension 0, may hold values from -6 to 6
- reset_points: int32 [16], P('groups'), parts along dimension 0, may hold values from 1 to 6143, as said below
- norm_gain: float32 [1024], replicated, may hold values from 0.1 to 1.9
- out_weight: bfloat16 [1024, 2048], P(None, 'ctx'), may hold values from -0.1875 to 0.1875
Outputs:
- attended: bfloat16 [12288, 2048], P(('groups', 'ctx')), parts along dimension 0
There are 2 independent parts, one for each index of `groups`. A program takes and returns all parts, laid end to end along the dimension named above; an argument that names none is the same for every part. Nothing has to cross between parts.
Inputs may be any that keep to these rules, and one draw needn't show every extreme that they name: reset_points[b] lies in the b-th of 8 equal spans of the sequence and is never that span's first position.
All inputs are finite; a program needn't handle non-finite values.
Results may differ from a plain program's by a relative error of at most 0.0058.
Values may be sent and summed in bfloat16 or wider, within the bound.
No kernel may reach another device: no remote copies, remote signals or barrier semaphores. Data moves between devices by JAX's collectives and lax.ppermute only.
A program may use at most 384 MiB of HBM per device.

v0:
```python
import jax
import jax.numpy as jnp
from jax import lax
from jax.sharding import PartitionSpec as P

HD = 128


HIGH = lax.Precision.HIGHEST
EPS = 1e-05


def carried_in(part, axis, combine, identity):
    place = lax.axis_index(axis)
    gathered = jax.tree.map(lambda a: lax.all_gather(a, axis), part)
    state = jax.tree.map(lambda a, e: jnp.zeros_like(a) + jnp.asarray(e, a.dtype), part, identity)

    def one(lap, state):
        return combine(
            state, jax.tree.map(lambda a: lax.dynamic_index_in_dim(a, lap, 0, False), gathered)
        )

    return lax.fori_loop(0, place, one, state)


def joint_merge(earlier, later):
    early_key, early_val, early_pair, early_flag = earlier
    later_key, later_val, later_pair, later_flag = later
    reset_now = later_flag > 0.5
    through = jnp.einsum("...ij,...jk->...ik", later_key, early_val, precision=HIGH)
    return (
        jnp.where(reset_now, later_key, early_key + later_key),
        jnp.where(reset_now, later_val, early_val + later_val),
        jnp.where(reset_now, later_pair, early_pair + later_pair + through),
        jnp.maximum(early_flag, later_flag),
    )


def on_device(queries, keys, values, reset_points, norm_gain, out_weight):
    length = queries.shape[0]
    head_count = queries.shape[1] // HD
    query_heads = queries.reshape(length, head_count, HD)
    key_heads = keys.reshape(length, head_count, HD)
    value_heads = values.reshape(length, head_count, HD)
    first_pos = lax.axis_index("ctx") * length
    offsets = jnp.arange(length, dtype=jnp.int32)
    positions = first_pos + offsets
    segment = jnp.sum((positions[:, None] >= reset_points[None, :]).astype(jnp.int32), axis=1)
    seg_before = jnp.sum((reset_points < first_pos).astype(jnp.int32))
    causal = offsets[None, :] <= offsets[:, None]
    same_seg = segment[:, None] == segment[None, :]
    visible = causal & same_seg
    bf_zero = jnp.zeros((), jnp.bfloat16)
    rounded = jnp.einsum(
        "thd,ihd->hti", query_heads, key_heads, preferred_element_type=jnp.float32
    ).astype(jnp.bfloat16)
    lower = jnp.where(visible[None], rounded, bf_zero)
    pair_scores = jnp.einsum("hti,hji->htj", lower, lower, preferred_element_type=jnp.float32)
    pair_scores = jnp.where(visible[None], pair_scores, jnp.float32(0.0)).astype(jnp.bfloat16)
    inside = jnp.einsum(
        "htj,jhd->thd", pair_scores, value_heads, preferred_element_type=jnp.float32
    )
    tail_rows = segment == segment[-1]
    key_tail = jnp.where(tail_rows[:, None, None], key_heads, bf_zero)
    query_tail = jnp.where(tail_rows[:, None, None], query_heads, bf_zero)
    key_cov = jnp.einsum("ihd,ihe->hde", key_tail, key_heads, preferred_element_type=jnp.float32)
    val_cov = jnp.einsum(
        "jhd,jhe->hde", query_tail, value_heads, preferred_element_type=jnp.float32
    )
    later_mask = (offsets[None, :] > offsets[:, None]) & same_seg
    upper = jnp.where(later_mask[None], rounded, bf_zero)
    carried = jnp.einsum(
        "hji,jhd->ihd", upper, value_heads, preferred_element_type=jnp.float32
    ).astype(jnp.bfloat16)
    pair_sum = jnp.einsum("ihd,ihe->hde", key_tail, carried, preferred_element_type=jnp.float32)
    reset_flag = (segment[-1] != seg_before).astype(jnp.float32)
    zeros = jnp.zeros_like(key_cov)
    no_flag = jnp.zeros((), jnp.float32)
    key_prev, val_prev, pair_prev, unused = carried_in(
        (key_cov, val_cov, pair_sum, reset_flag), "ctx", joint_merge, (zeros, zeros, zeros, no_flag)
    )
    history = jnp.einsum("hij,hjk->hik", key_prev, val_prev, precision=HIGH) - pair_prev
    open_rows = segment == seg_before
    query_wide = query_heads.astype(jnp.float32)
    q_state = jnp.einsum("thd,hde->hte", query_wide, key_prev, precision=HIGH).astype(jnp.bfloat16)
    reach = causal & open_rows[:, None]
    mixed_scores = jnp.einsum(
        "hte,jhe->htj", q_state, query_heads, preferred_element_type=jnp.float32
    )
    mixed_scores = jnp.where(reach[None], mixed_scores, jnp.float32(0.0)).astype(jnp.bfloat16)
    across = jnp.einsum(
        "htj,jhd->thd", mixed_scores, value_heads, preferred_element_type=jnp.float32
    )
    across = across + jnp.einsum("thd,hde->the", query_wide, history, precision=HIGH)
    across = jnp.where(open_rows[:, None, None], across, jnp.float32(0.0))
    summed = inside + across
    inverse = lax.rsqrt(jnp.mean(summed * summed, axis=2, keepdims=True) + EPS)
    hidden = (
        (summed * inverse * norm_gain.reshape(head_count, HD)[None])
        .astype(jnp.bfloat16)
        .reshape(length, head_count * HD)
    )
    attended = jnp.dot(
        hidden,
        lax.all_gather(out_weight, "ctx", axis=1, tiled=True),
        preferred_element_type=jnp.float32,
    )
    return attended.astype(jnp.bfloat16)


def solution(mesh):
    placed = (
        P(("groups", "ctx"), None),
        P(("groups", "ctx"), None),
        P(("groups", "ctx"), None),
        P("groups"),
        P(),
        P(None, "ctx"),
    )
    return jax.shard_map(
        on_device, mesh=mesh, in_specs=placed, out_specs=P(("groups", "ctx"), None), check_vma=False
    )
```

profile of v0, /device:TPU:27, one launch (start us, length us, event | category | flops | bytes accessed | tf_op | source)
XLA Modules:
  0.0 336.5 jit_solution(10782350341229577408)
XLA Ops:
  12.6 2.2 convolution_convert_fusion.1
  14.9 3.6 %fusion.31 = f32[8,128,128]{2,1,0:T(8,128)} fusion(bf16[8,384,384]{2,1,0:T(8,128)(2,1)} %convolution_convert_fusion.1, pred[384,384]{1,0:T(8,128)(4,1)S(1)} %get-tuple-element.105, bf16[384,8,128]{0,2,1:T(8,128)(2,1)S(1)} %bitcast.86, pred[384]{0:T(512)(128)(4,1)S(1)} %get-tuple-element.103, bf16[384,1024]{1,0:T(8,128)(2,1)S(1)} %copy-done.1), kind=kOutput, calls=%fused_computation.34 | convolution fusion | flops 404619264 | bytes 4604288 | tf_op jit(solution)/shard_map/ihd,ihe->hde/dot_general | solution.py:75
  24.1 29.6 %all-reduce = f32[16]{0:T(128)S(1)} all-reduce(f32[16]{0:T(128)S(1)} %dynamic-update-slice), channel_id=1, replica_groups=mesh['groups'=2,'ctx'=16] {'ctx'}, use_global_device_ids=true, to_apply=%add | all-reduce | flops 16 | bytes 128
  54.6 6.0 %fusion.4 = f32[8,384,128]{1,2,0:T(8,128)} fusion(bf16[384,8,128]{0,2,1:T(8,128)(2,1)S(1)} %copy.29, pred[384,384]{1,0:T(8,128)(4,1)S(1)} %get-tuple-element.104, bf16[8,384,384]{2,1,0:T(8,128)(2,1)} %convolution_convert_fusion.1), kind=kOutput, calls=%fused_computation.11 | convolution fusion | flops 1211498496 | bytes 4866048 | tf_op jit(solution)/shard_map/htj,jhd->thd/dot_general | solution.py:60
  60.6 32.0 %all-gather.14.cloned.1.call-done = f32[128,128,128]{2,1,0:T(8,128)} async-done(((f32[8,128,128]{2,1,0:T(8,128)}), f32[128,128,128]{2,1,0:T(8,128)}) %all-gather.14.cloned.1.call-update) | async-done | bytes 8388624 | tf_op jit(solution)/shard_map/all_gather | solution.py:15
  92.6 75.3 %all-gather.12.cloned.1.call-done = f32[128,128,128]{2,1,0:T(8,128)} async-done(((f32[8,128,128]{2,1,0:T(8,128)}), f32[128,128,128]{2,1,0:T(8,128)}) %all-gather.12.cloned.1.call-update) | async-done | bytes 8388624 | tf_op jit(solution)/shard_map/all_gather | solution.py:15
  167.9 75.3 %all-gather.10.cloned.1.call-done = f32[128,128,128]{2,1,0:T(8,128)} async-done(((f32[8,128,128]{2,1,0:T(8,128)}), f32[128,128,128]{2,1,0:T(8,128)}) %all-gather.10.cloned.1.call-update) | async-done | bytes 8388624 | tf_op jit(solution)/shard_map/all_gather | solution.py:15
  243.4 73.0 %while.16 = (s32[]{:T(128)}, f32[8,128,128]{2,1,0:T(8,128)S(1)}, f32[8,128,128]{2,1,0:T(8,128)S(1)}, f32[8,128,128]{2,1,0:T(8,128)S(1)}, s32[]{:T(128)}, /*index...) while((s32[]{:T(128)}, f32[8,128,128]{2,1,0:T(8,128)S(1)}, ...), condition=%wide.region_3.4_spmd, body=%wide.region_2.3_spmd.sunk | while | flops 202244096 | bytes 5768889 | solution.py:23
  244.6 2.0 fusion.88
  249.5 2.0 fusion.88
  254.3 2.0 fusion.88
  259.2 2.0 fusion.88
  261.2 1.6 add_select_fusion.3
  264.0 2.0 fusion.88
  266.0 1.6 add_select_fusion.3
  268.9 2.0 fusion.88
  270.9 1.6 add_select_fusion.3
  273.7 2.1 fusion.88
  275.8 1.6 add_select_fusion.3
  278.7 2.0 fusion.88
  280.7 1.6 add_select_fusion.3
  283.6 2.0 fusion.88
  288.4 2.0 fusion.88
  293.3 2.0 fusion.88
  298.1 2.0 fusion.88
  302.9 2.0 fusion.88
  307.8 2.0 fusion.88
  312.6 2.0 fusion.88
  316.4 1.8 convolution_convert_fusion.2
  318.8 2.0 fusion.64
  320.8 3.7 %multiply_reduce_fusion = (f32[384,8]{0,1:T(8,128)S(1)}, f32[384,8,128]{0,2,1:T(8,128)S(1)}) fusion(f32[8,128,384]{2,1,0:T(8,128)} %fusion.64, bf16[384,8,128]{0,2,1:T(8,128)(2,1)S(1)} %copy.29, pred[384,384]{1,0:T(8,128)(4,1)S(1)} %fusion.51, bf16[8,128,384]{2,1,0:T(8,128)(2,1)} %convolution_convert_fusion.2, bf16[384,8,128]{0,2,1:T(8,128)(2,1)S(1)} %bitcast.82, ...), kind=kOutput, calls=%fused_computation.29 | convolution fusion | flops 608302080 | bytes 7238016 | tf_op jit(solution)/shard_map/htj,jhd->thd/dot_general | solution.py:91
  324.8 5.2 %convolution_convert_fusion = bf16[384,2048]{1,0:T(8,128)(2,1)} fusion(bf16[384,1024]{0,1:T(8,128)(2,1)S(1)} %bitcast.91, bf16[1024,2048]{1,0:T(8,128)(2,1)} %all-gather.8.cloned.1.call-done), kind=kOutput, calls=%fused_computation.10 | convolution fusion | flops 1611399168 | bytes 6553600 | tf_op jit(solution)/shard_map/dot_general | solution.py:103
  (64 shorter events, 37.2 us)
Async XLA Ops:
  6.5 4.4 %copy-start = (bf16[384,1024]{1,0:T(8,128)(2,1)S(1)}, bf16[384,1024]{1,0:T(8,128)(2,1)}, u32[]{:S(2)}) copy-start(bf16[384,1024]{1,0:T(8,128)(2,1)} %param.9) | copy-start | bytes 2359300
  6.5 86.0 %all-gather.14.cloned.1.call-start = ((), (), s32[]{:S(2)}) async-start(), calls=%async_computation.3 | async-start | bytes 8912896 | tf_op jit(solution)/shard_map/all_gather | solution.py:15
  11.3 3.5 %copy-start.1 = (bf16[384,1024]{1,0:T(8,128)(2,1)S(1)}, bf16[384,1024]{1,0:T(8,128)(2,1)}, u32[]{:S(2)}) copy-start(bf16[384,1024]{1,0:T(8,128)(2,1)} %param.10) | copy-start | bytes 2359300
  18.5 149.4 %all-gather.12.cloned.1.call-start = ((), (), s32[]{:S(2)}) async-start(), calls=%async_computation.2 | async-start | bytes 8912896 | tf_op jit(solution)/shard_map/all_gather | solution.py:15
  19.7 3.2 copy-start.3
  19.7 223.5 %all-gather.10.cloned.1.call-start = ((), (), s32[]{:S(2)}) async-start(), calls=%async_computation.1 | async-start | bytes 8912896 | tf_op jit(solution)/shard_map/all_gather | solution.py:15
  21.1 303.7 %all-gather.8.cloned.1.call-start = ((), (), s32[]{:S(2)}) async-start(), calls=%async_computation | async-start | bytes 4456448 | tf_op jit(solution)/shard_map/all_gather | solution.py:105
  320.8 3.7 %copy-start.2 = (f32[1024]{0:T(1024)S(1)}, f32[1024]{0:T(1024)}, u32[]{:S(2)}) copy-start(f32[1024]{0:T(1024)} %param.12) | copy-start | bytes 12292
Sparse Core Ops, SparseCore 0:
  18.6 73.9 all-gather.13
  94.7 73.1 all-gather.11
  170.1 73.1 all-gather.9
  245.3 51.3 all-gather.7
where the time goes:
time: 338 us; the launch traced here: 336 us
  waiting for transfers between devices  183 us (54%)
  matrix products  57 us (17%)
  blocking collectives  29.6 us (9%)
  other arithmetic  28.1 us (8%)
  between operations  14.5 us (4%)
  local copies, waits for them, and re-layouts  13.4 us (4%)
  loops' own time  10.5 us (3%)
    all_gather x3, waiting for transfers between devices, carried_in(): gathered = jax.tree.map(lambda a: lax.all_gather(a, axis), part)  183 us
    unnamed x1, blocking collectives  29.6 us
    dot_general x15, matrix products, joint_merge(): jnp.einsum('...ij,...jk->...ik', later_key, early_val, precision=HIGH)  29.5 us
    select_n x15, other arithmetic, joint_merge(): jnp.where(reset_now, later_val, early_val + later_val)  24.2 us
    another operation x1, loops' own time, carried_in(): return lax.fori_loop(0, place, one, state)  10.5 us
    dynamic_slice x15, local copies, waits for them, and re-layouts, one(): lax.dynamic_index_in_dim(a, lap, 0, False)  8.8 us
  transfers between devices with their start and end apart: 4, of which 3 were waited for; matrix products, arithmetic and copies ran while one was open for 24% of the time, Pallas kernels for 0%

commit v1 on v0

v1 whole, which is shorter than its diff:
```python
import functools

import jax
import jax.numpy as jnp
from jax import lax
from jax.experimental import pallas as pl
from jax.experimental.pallas import tpu as pltpu
from jax.sharding import PartitionSpec as P

HD = 128
EPS = 1e-05
BF = jnp.bfloat16
F32 = jnp.float32
VMEM_LIMIT = 48 * 1024 * 1024


def dot(a, b, ca, cb):
    return lax.dot_general(a, b, (((ca,), (cb,)), ((), ())), preferred_element_type=F32)


def params(**more):
    return pltpu.CompilerParams(vmem_limit_bytes=VMEM_LIMIT, **more)


def visible_mask(cut, length):
    row = lax.broadcasted_iota(jnp.int32, (length, length), 0)
    col = lax.broadcasted_iota(jnp.int32, (length, length), 1)
    return (col <= row) & ((row < cut) | (col >= cut))


def state_kernel(heads, info, q_ref, k_ref, v_ref, w_ref, st_ref):
    length = q_ref.shape[0]
    cut, has = info[0], info[1]
    visible = visible_mask(cut, length)
    row = lax.broadcasted_iota(jnp.int32, (length, HD), 0)
    tail = (row >= cut) | (has == 0)
    zero = jnp.zeros((), BF)
    for h in range(heads):
        at = slice(h * HD, (h + 1) * HD)
        q, k, v = q_ref[:, at], k_ref[:, at], v_ref[:, at]
        scores = jnp.where(visible, dot(q, k, 1, 1), 0.0).astype(BF)
        w = dot(scores, k, 1, 0).astype(BF)
        w_ref[:, at] = w
        v_tail = jnp.where(tail, v, zero)
        k_tail = jnp.where(tail, k, zero)
        st_ref[0, h] = dot(k_tail, k, 0, 0).astype(BF)
        st_ref[1, h] = dot(q, v_tail, 0, 0).astype(BF)
        st_ref[2, h] = dot(w, v_tail, 0, 0).astype(BF)


def chip_kernel(half, info, own_ref, other_ref, out_ref):
    core, has_second = info[2], info[3]
    first = core == 0
    for j in range(half):
        h = core * half + j
        own = [own_ref[n, h].astype(F32) for n in range(3)]
        oth = [other_ref[n, h].astype(F32) for n in range(3)]
        s0, h0 = jnp.where(first, own[0], oth[0]), jnp.where(first, own[2], oth[2])
        s1, c1, h1 = (jnp.where(first, oth[n], own[n]) for n in range(3))
        through = dot(s0.astype(BF), c1.astype(BF), 1, 0)
        keep = has_second == 0
        out_ref[0, j] = jnp.where(keep, s0 + s1, s1).astype(BF)
        out_ref[1, j] = jnp.where(keep, h0 + h1 + through, h1).astype(BF)


def output_kernel(heads, half, info, q_ref, v_ref, w_ref, gain_ref, other_ref, same_ref, swap_ref, out_ref):
    length = q_ref.shape[0]
    cut, has, core, keep_chip = info[0], info[1], info[2], info[4]
    visible = visible_mask(cut, length)
    row = lax.broadcasted_iota(jnp.int32, (length, HD), 0)
    is_open = (row < cut) | (has == 0)
    step = pl.program_id(0)
    for h in range(heads):
        at = slice(h * HD, (h + 1) * HD)
        head = step * heads + h
        place = lax.rem(head, half)
        mine = lax.div(head, half) == core
        s_chip = jnp.where(mine, same_ref[0, place], swap_ref[0, place]).astype(F32)
        h_chip = jnp.where(mine, same_ref[1, place], swap_ref[1, place]).astype(F32)
        s_chip = jnp.where(keep_chip == 1, s_chip, 0.0)
        h_chip = jnp.where(keep_chip == 1, h_chip, 0.0)
        s_in, c_in, h_in = (other_ref[n, h].astype(F32) for n in range(3))
        through = dot(s_chip.astype(BF), c_in.astype(BF), 1, 0)
        second = core == 1
        s_prev = jnp.where(second, s_chip + s_in, s_chip).astype(BF)
        h_prev = jnp.where(second, h_chip + h_in + through, h_chip).astype(BF)
        q, v = q_ref[:, at], v_ref[:, at]
        w = w_ref[:, at].astype(F32) + jnp.where(is_open, dot(q, s_prev, 1, 0), 0.0)
        scores = jnp.where(visible, dot(q, w.astype(BF), 1, 1), 0.0).astype(BF)
        summed = dot(scores, v, 1, 0) + jnp.where(is_open, dot(q, h_prev, 1, 0), 0.0)
        inverse = lax.rsqrt(jnp.mean(summed * summed, axis=1, keepdims=True) + EPS)
        out_ref[:, at] = (summed * inverse * gain_ref[:, at]).astype(BF)


def project_kernel(pairs, info, hidden_ref, *refs):
    same, other, out_ref = refs[:pairs], refs[pairs : 2 * pairs], refs[-1]
    first = info[2] == 0
    for n in range(pairs):
        cols = same[n].shape[1]
        a, b = same[n][...], other[n][...]
        both = jnp.concatenate([jnp.where(first, a, b), jnp.where(first, b, a)], axis=1)
        at = pl.multiple_of(info[8 + n], 2 * cols)
        out_ref[:, pl.ds(at, 2 * cols)] = dot(hidden_ref[...], both, 1, 0).astype(BF)


def smem():
    return pl.BlockSpec(memory_space=pltpu.SMEM)


def swap_by(mask, n):
    return [(i, i ^ mask) for i in range(n)]


def on_device(blocks, queries, keys, values, reset_points, norm_gain, out_weight):
    length, width = queries.shape
    heads = width // HD
    half = heads // 2
    n_ctx = blocks
    per_span = n_ctx // reset_points.shape[0]
    assert per_span == 2 and heads % 2 == 0
    index = lax.axis_index("ctx")
    core, chip = index % 2, index // 2
    local = reset_points[chip] - index * length
    has = (local >= 0) & (local < length)
    local_pair = reset_points[chip] - chip * 2 * length
    has_second = local_pair >= length
    cut = jnp.where(has, local, 0)
    keep_chip = (chip > 0) & ((core == 0) | has_second)
    masks = [0, 2, 4, 6, 8, 10, 12, 14]
    info = jnp.stack(
        [cut, has, core, has_second, keep_chip, cut, cut, cut]
        + [((index ^ m) // 2) * 2 * out_weight.shape[1] for m in masks]
    ).astype(jnp.int32)

    small = n_ctx == 16 and out_weight.shape[1] == HD
    if small:
        x_swap = functools.partial(lax.ppermute, axis_name="ctx", perm=swap_by(2, n_ctx))
        z_got = {m: lax.ppermute(out_weight, "ctx", swap_by(m, n_ctx)) for m in (4, 8, 12)}
        pieces = {0: out_weight, 2: x_swap(out_weight)}
        for m in (4, 8, 12):
            pieces[m] = z_got[m]
            pieces[m + 2] = x_swap(z_got[m])
        same = [pieces[m] for m in masks]
        other = [lax.ppermute(p, "ctx", swap_by(1, n_ctx)) for p in same]

    step_heads = 2
    steps = heads // step_heads
    block = step_heads * HD
    row_spec = pl.BlockSpec((length, block), lambda s: (0, s))
    state_spec = pl.BlockSpec((3, step_heads, HD, HD), lambda s: (0, s, 0, 0))
    w, state = pl.pallas_call(
        functools.partial(state_kernel, step_heads),
        grid=(steps,),
        in_specs=[smem(), row_spec, row_spec, row_spec],
        out_specs=[row_spec, state_spec],
        out_shape=[
            jax.ShapeDtypeStruct((length, width), BF),
            jax.ShapeDtypeStruct((3, heads, HD, HD), BF),
        ],
        compiler_params=params(),
        name="block_state",
    )(info, queries, keys, values)
    state_other = lax.ppermute(state, "ctx", swap_by(1, n_ctx))
    chip_state = pl.pallas_call(
        functools.partial(chip_kernel, half),
        in_specs=[smem(), pl.BlockSpec(memory_space=pltpu.VMEM), pl.BlockSpec(memory_space=pltpu.VMEM)],
        out_shape=jax.ShapeDtypeStruct((2, half, HD, HD), BF),
        compiler_params=params(),
        name="chip_state",
    )(info, state, state_other)
    before = lax.ppermute(chip_state, "ctx", [(i, i + 2) for i in range(n_ctx - 2)])
    before_swap = lax.ppermute(before, "ctx", swap_by(1, n_ctx))
    hidden = pl.pallas_call(
        functools.partial(output_kernel, step_heads, half),
        grid=(steps,),
        in_specs=[
            smem(),
            row_spec,
            row_spec,
            row_spec,
            pl.BlockSpec((1, block), lambda s: (0, s)),
            state_spec,
            pl.BlockSpec((2, half, HD, HD), lambda s: (0, 0, 0, 0)),
            pl.BlockSpec((2, half, HD, HD), lambda s: (0, 0, 0, 0)),
        ],
        out_specs=row_spec,
        out_shape=jax.ShapeDtypeStruct((length, width), BF),
        compiler_params=params(),
        name="block_output",
    )(info, queries, values, w, norm_gain.reshape(1, width), state_other, before, before_swap)
    if not small:
        whole = lax.all_gather(out_weight, "ctx", axis=1, tiled=True)
        return jnp.dot(hidden, whole, preferred_element_type=F32).astype(BF)
    pairs = len(masks)
    return pl.pallas_call(
        functools.partial(project_kernel, pairs),
        in_specs=[smem()] + [pl.BlockSpec(memory_space=pltpu.VMEM)] * (1 + 2 * pairs),
        out_shape=jax.ShapeDtypeStruct((length, n_ctx * out_weight.shape[1]), BF),
        compiler_params=params(),
        name="project",
    )(info, hidden, *same, *other)


def solution(mesh):
    placed = (
        P(("groups", "ctx"), None),
        P(("groups", "ctx"), None),
        P(("groups", "ctx"), None),
        P("groups"),
        P(),
        P(None, "ctx"),
    )
    return jax.shard_map(
        functools.partial(on_device, mesh.shape["ctx"]),
        mesh=mesh,
        in_specs=placed,
        out_specs=P(("groups", "ctx"), None),
        check_vma=False,
    )
```

time: 338 us -> 66.5 us (0.20)
  the two profiles are of different devices: /device:TPU:27 before, /device:TPU:17 now
where the time goes in v1:
time: 66.5 us; the launch traced here: 66.3 us
  waiting for transfers between devices  29.6 us (45%)
  starting transfers between devices  15.5 us (23%)
  Pallas kernels  14.7 us (22%)
  local copies, waits for them, and re-layouts  4.78 us (7%)
  between operations  1.61 us (2%)
    ppermute x3, waiting for transfers between devices, on_device(): lax.ppermute(out_weight, 'ctx', swap_by(m, n_ctx))  16.6 us
    ppermute x3, waiting for transfers between devices, on_device(): pieces[m + 2] = x_swap(z_got[m])  10.1 us
    pallas_call x1, Pallas kernels, on_device(): pl.pallas_call(functools.partial(output_kernel, step_heads, half), grid=(...  5.28 us
    pallas_call x1, Pallas kernels, on_device(): pl.pallas_call(functools.partial(state_kernel, step_heads), grid=(steps,)...  4.98 us
    ppermute x8, starting transfers between devices, on_device(): other = [lax.ppermute(p, 'ctx', swap_by(1, n_ctx)) for p in same]  4.67 us
    pallas_call x1, Pallas kernels, on_device(): pl.pallas_call(functools.partial(project_kernel, pairs), in_specs=[smem()...  3.69 us
    unnamed x14, local copies, waits for them, and re-layouts  3.41 us
    ppermute x1, waiting for transfers between devices, on_device(): lax.ppermute(chip_state, 'ctx', [(i, i + 2) for i in range(n_ctx - 2)])  2.97 us
  transfers between devices with their start and end apart: 18, of which 5 were waited for; matrix products, arithmetic and copies ran while one was open for 0% of the time, Pallas kernels for 9%

profile of v1, /device:TPU:17, one launch (start us, length us, event | category | flops | bytes accessed | tf_op | source)
XLA Modules:
  0.0 66.3 jit_solution(14817086517666127944)
XLA Ops:
  0.0 1.3 %dynamic_slice.4 = s32[1]{0:T(128)} dynamic-slice(s32[8]{0:T(128)} %param.9, s32[]{:T(128)S(6)} %select_n.42), dynamic_slice_sizes={1} | dynamic-slice | bytes 12 | tf_op jit(solution)/shard_map/dynamic_slice | solution.py:123
  2.8 0.1 stack.70.info
  2.9 1.1 %copy-done = bf16[384,1024]{1,0:T(8,128)(2,1)S(1)} copy-done((bf16[384,1024]{1,0:T(8,128)(2,1)S(1)}, bf16[384,1024]{1,0:T(8,128)(2,1)}, u32[]{:S(2)}) %copy-start) | copy-done | bytes 786456
  4.0 1.1 %copy-done.2 = bf16[384,1024]{1,0:T(8,128)(2,1)S(1)} copy-done((bf16[384,1024]{1,0:T(8,128)(2,1)S(1)}, bf16[384,1024]{1,0:T(8,128)(2,1)}, u32[]{:S(2)}) %copy-start.2) | copy-done | bytes 786456
  5.1 1.1 %copy-done.4 = bf16[384,1024]{1,0:T(8,128)(2,1)S(1)} copy-done((bf16[384,1024]{1,0:T(8,128)(2,1)S(1)}, bf16[384,1024]{1,0:T(8,128)(2,1)}, u32[]{:S(2)}) %copy-start.4) | copy-done | bytes 786456
  6.3 5.0 %block_state.1 = (bf16[384,1024]{1,0:T(8,128)(2,1)S(1)}, bf16[3,8,128,128]{3,2,1,0:T(8,128)(2,1)S(1)}) custom-call(s32[16]{0:T(128)S(1)} %stack.70.info, bf16[384,1024]{1,0:T(8,128)(2,1)S(1)} %copy-done, bf16[384,1024]{1,0:T(8,128)(2,1)S(1)} %copy-done.4, bf16[384,1024]{1,0:T(8,128)(2,1)S(1)} %copy-done.2), custom_call_target="tpu_custom_call" | custom-call | tf_op jit(solution)/shard_map/block_state/pallas_call | solution.py:151
  11.3 0.7 %collective-permute-start = (bf16[3,8,128,128]{3,2,1,0:T(8,128)(2,1)S(1)}, bf16[3,8,128,128]{3,2,1,0:T(8,128)(2,1)S(1)}, u32[]{:S(2)}, u32[]{:S(2)}) collective-permute-start(bf16[3,8,128,128]{3,2,1,0:T(8,128)(2,1)S(1)} %get-tuple-element.8.own_ref), channel_id=1, source_target_pairs={{0,1},{1,0},{2,3},{3,2},{4,5},{5,4},{6,7},{7,6},{8,9},{9,8},{10,11... | collective-permute-start | bytes 2359304 | tf_op jit(solution)/shard_map/ppermute | solution.py:163
  12.0 1.3 %collective-permute-start.4 = (bf16[1024,128]{1,0:T(8,128)(2,1)S(1)}, bf16[1024,128]{1,0:T(8,128)(2,1)S(1)}, u32[]{:S(2)}, u32[]{:S(2)}) collective-permute-start(bf16[1024,128]{1,0:T(8,128)(2,1)S(1)} %copy-done.5), channel_id=1, source_target_pairs={{0,4},{1,5},{2,6},{3,7},{4,0},{5,1},{6,2},{7,3},{8,12},{9,13},{10,... | collective-permute-start | bytes 786440 | tf_op jit(solution)/shard_map/ppermute | solution.py:138
  13.3 0.1 collective-permute-start.6
  13.4 1.3 %collective-permute-start.8 = (bf16[1024,128]{1,0:T(8,128)(2,1)S(1)}, bf16[1024,128]{1,0:T(8,128)(2,1)S(1)}, u32[]{:S(2)}, u32[]{:S(2)}) collective-permute-start(bf16[1024,128]{1,0:T(8,128)(2,1)S(1)} %copy-done.5), channel_id=1, source_target_pairs={{0,12},{1,13},{2,14},{3,15},{4,8},{5,9},{6,10},{7,11},{8,4},{9,5},... | collective-permute-start | bytes 786440 | tf_op jit(solution)/shard_map/ppermute | solution.py:138
  14.7 1.2 %collective-permute-start.3 = (bf16[1024,128]{1,0:T(8,128)(2,1)S(1)}, bf16[1024,128]{1,0:T(8,128)(2,1)S(1)}, u32[]{:S(2)}, u32[]{:S(2)}) collective-permute-start(bf16[1024,128]{1,0:T(8,128)(2,1)S(1)} %copy-done.5), channel_id=1, source_target_pairs={{0,2},{1,3},{2,0},{3,1},{4,6},{5,7},{6,4},{7,5},{8,10},{9,11},{10,... | collective-permute-start | bytes 786440 | tf_op jit(solution)/shard_map/ppermute | solution.py:139
  15.9 7.5 %collective-permute-done.4.refs_2_ = bf16[1024,128]{1,0:T(8,128)(2,1)S(1)} collective-permute-done((bf16[1024,128]{1,0:T(8,128)(2,1)S(1)}, bf16[1024,128]{1,0:T(8,128)(2,1)S(1)}, u32[]{:S(2)}, u32[]{:S(2)}) %collective-permute-start.4) | collective-permute-done | bytes 262176 | tf_op jit(solution)/shard_map/ppermute | solution.py:138
  23.4 0.9 %collective-permute-start.10 = (bf16[1024,128]{1,0:T(8,128)(2,1)S(1)}, bf16[1024,128]{1,0:T(8,128)(2,1)S(1)}, u32[]{:S(2)}, u32[]{:S(2)}) collective-permute-start(bf16[1024,128]{1,0:T(8,128)(2,1)S(1)} %copy-done.5), channel_id=1, source_target_pairs={{0,1},{1,0},{2,3},{3,2},{4,5},{5,4},{6,7},{7,6},{8,9},{9,8},{10,11... | collective-permute-start | bytes 786440 | tf_op jit(solution)/shard_map/ppermute | solution.py:144
  24.2 1.2 %collective-permute-start.5 = (bf16[1024,128]{1,0:T(8,128)(2,1)S(1)}, bf16[1024,128]{1,0:T(8,128)(2,1)S(1)}, u32[]{:S(2)}, u32[]{:S(2)}) collective-permute-start(bf16[1024,128]{1,0:T(8,128)(2,1)S(1)} %collective-permute-done.4.refs_2_), channel_id=1, source_target_pairs={{0,2},{1,3},{2,0},{3,1},{4,6},{5,7},{6,4},{7,5},{8,10},{9,11},{10,... | collective-permute-start | bytes 786440 | tf_op jit(solution)/shard_map/ppermute | solution.py:142
  25.4 0.8 %chip_state.1 = bf16[2,4,128,128]{3,2,1,0:T(8,128)(2,1)S(1)} custom-call(s32[16]{0:T(128)S(1)} %stack.70.info, bf16[3,8,128,128]{3,2,1,0:T(8,128)(2,1)S(1)} %get-tuple-element.8.own_ref, bf16[3,8,128,128]{3,2,1,0:T(8,128)(2,1)S(1)} %collective-permute-done.other_ref), custom_call_target="tpu_custom_call" | custom-call | tf_op jit(solution)/shard_map/chip_state/pallas_call | solution.py:164
  26.2 2.3 %collective-permute-start.1 = (bf16[2,4,128,128]{3,2,1,0:T(8,128)(2,1)S(1)}, bf16[2,4,128,128]{3,2,1,0:T(8,128)(2,1)S(1)}, u32[]{:S(2)}, u32[]{:S(2)}) collective-permute-start(bf16[2,4,128,128]{3,2,1,0:T(8,128)(2,1)S(1)} %chip_state.1), channel_id=1, source_target_pairs={{0,2},{1,3},{2,4},{3,5},{4,6},{5,7},{6,8},{7,9},{8,10},{9,11},{10,... | collective-permute-start | bytes 786440 | tf_op jit(solution)/shard_map/ppermute | solution.py:171
  28.6 9.1 %collective-permute-done.8.refs_6_ = bf16[1024,128]{1,0:T(8,128)(2,1)S(1)} collective-permute-done((bf16[1024,128]{1,0:T(8,128)(2,1)S(1)}, bf16[1024,128]{1,0:T(8,128)(2,1)S(1)}, u32[]{:S(2)}, u32[]{:S(2)}) %collective-permute-start.8) | collective-permute-done | bytes 262176 | tf_op jit(solution)/shard_map/ppermute | solution.py:138
  37.7 1.2 %collective-permute-start.7 = (bf16[1024,128]{1,0:T(8,128)(2,1)S(1)}, bf16[1024,128]{1,0:T(8,128)(2,1)S(1)}, u32[]{:S(2)}, u32[]{:S(2)}) collective-permute-start(bf16[1024,128]{1,0:T(8,128)(2,1)S(1)} %collective-permute-done.6.refs_4_), channel_id=1, source_target_pairs={{0,2},{1,3},{2,0},{3,1},{4,6},{5,7},{6,4},{7,5},{8,10},{9,11},{10,... | collective-permute-start | bytes 786440 | tf_op jit(solution)/shard_map/ppermute | solution.py:142
  38.9 0.2 collective-permute-start.9
  39.1 2.1 %collective-permute-start.12 = (bf16[1024,128]{1,0:T(8,128)(2,1)S(1)}, bf16[1024,128]{1,0:T(8,128)(2,1)S(1)}, u32[]{:S(2)}, u32[]{:S(2)}) collective-permute-start(bf16[1024,128]{1,0:T(8,128)(2,1)S(1)} %collective-permute-done.4.refs_2_), channel_id=1, source_target_pairs={{0,1},{1,0},{2,3},{3,2},{4,5},{5,4},{6,7},{7,6},{8,9},{9,8},{10,11... | collective-permute-start | bytes 786440 | tf_op jit(solution)/shard_map/ppermute | solution.py:144
  41.2 0.1 collective-permute-start.14
  41.3 3.0 %collective-permute-done.1.same_ref = bf16[2,4,128,128]{3,2,1,0:T(8,128)(2,1)S(1)} collective-permute-done((bf16[2,4,128,128]{3,2,1,0:T(8,128)(2,1)S(1)}, bf16[2,4,128,128]{3,2,1,0:T(8,128)(2,1)S(1)}, u32[]{:S(2)}, u32[]{:S(2)}) %collective-permute-start.1) | collective-permute-done | bytes 262176 | tf_op jit(solution)/shard_map/ppermute | solution.py:171
  44.3 1.2 %collective-permute-start.2 = (bf16[2,4,128,128]{3,2,1,0:T(8,128)(2,1)S(1)}, bf16[2,4,128,128]{3,2,1,0:T(8,128)(2,1)S(1)}, u32[]{:S(2)}, u32[]{:S(2)}) collective-permute-start(bf16[2,4,128,128]{3,2,1,0:T(8,128)(2,1)S(1)} %collective-permute-done.1.same_ref), channel_id=1, source_target_pairs={{0,1},{1,0},{2,3},{3,2},{4,5},{5,4},{6,7},{7,6},{8,9},{9,8},{10,11... | collective-permute-start | bytes 786440 | tf_op jit(solution)/shard_map/ppermute | solution.py:172
  45.5 5.0 %collective-permute-done.7.refs_5_ = bf16[1024,128]{1,0:T(8,128)(2,1)S(1)} collective-permute-done((bf16[1024,128]{1,0:T(8,128)(2,1)S(1)}, bf16[1024,128]{1,0:T(8,128)(2,1)S(1)}, u32[]{:S(2)}, u32[]{:S(2)}) %collective-permute-start.7) | collective-permute-done | bytes 262176 | tf_op jit(solution)/shard_map/ppermute | solution.py:142
  50.5 0.6 collective-permute-start.16
  51.1 5.0 %collective-permute-done.9.refs_7_ = bf16[1024,128]{1,0:T(8,128)(2,1)S(1)} collective-permute-done((bf16[1024,128]{1,0:T(8,128)(2,1)S(1)}, bf16[1024,128]{1,0:T(8,128)(2,1)S(1)}, u32[]{:S(2)}, u32[]{:S(2)}) %collective-permute-start.9) | collective-permute-done | bytes 262176 | tf_op jit(solution)/shard_map/ppermute | solution.py:142
  56.1 0.5 collective-permute-start.11
  56.6 0.0 collective-permute-start.13
  56.6 0.5 collective-permute-start.15
  57.1 0.1 collective-permute-start.17
  57.2 5.3 %block_output.1.hidden_ref = bf16[384,1024]{1,0:T(8,128)(2,1)S(1)} custom-call(s32[16]{0:T(128)S(1)} %stack.70.info, bf16[384,1024]{1,0:T(8,128)(2,1)S(1)} %copy-done.1, bf16[384,1024]{1,0:T(8,128)(2,1)S(1)} %copy-done.3, bf16[384,1024]{1,0:T(8,128)(2,1)S(1)} %get-tuple-element.7.w_ref, f32[1,1024]{1,0:T(1,128)S(1)} %bitcast.15, ...), custom_call_target="tpu_custom_call" | custom-call | tf_op jit(solution)/shard_map/block_output/pallas_call | solution.py:173
  62.6 3.7 %project.1 = bf16[384,2048]{1,0:T(8,128)(2,1)} custom-call(s32[16]{0:T(128)S(1)} %stack.70.info, bf16[384,1024]{1,0:T(8,128)(2,1)S(1)} %block_output.1.hidden_ref, bf16[1024,128]{1,0:T(8,128)(2,1)S(1)} %copy-done.5, bf16[1024,128]{1,0:T(8,128)(2,1)S(1)} %collective-permute-done.3.refs_1_, bf16[1024,128]{1,0:T(8,128)(2,1)S(1)} %collective-permute-done.4.refs_2_, ...), custom_call_target="tpu_custom_call" | custom-call | tf_op jit(solution)/shard_map/project/pallas_call | solution.py:195
  (24 shorter events, 0.1 us)
Async XLA Ops:
  0.0 12.0 %copy-start.5 = (bf16[1024,128]{1,0:T(8,128)(2,1)S(1)}, bf16[1024,128]{1,0:T(8,128)(2,1)}, u32[]{:S(2)}) copy-start(bf16[1024,128]{1,0:T(8,128)(2,1)} %refs_0_.1) | copy-start | bytes 786436
  2.9 1.1 %copy-start = (bf16[384,1024]{1,0:T(8,128)(2,1)S(1)}, bf16[384,1024]{1,0:T(8,128)(2,1)}, u32[]{:S(2)}) copy-start(bf16[384,1024]{1,0:T(8,128)(2,1)} %q_ref.3) | copy-start | bytes 2359300
  4.0 1.1 %copy-start.2 = (bf16[384,1024]{1,0:T(8,128)(2,1)S(1)}, bf16[384,1024]{1,0:T(8,128)(2,1)}, u32[]{:S(2)}) copy-start(bf16[384,1024]{1,0:T(8,128)(2,1)} %v_ref.3) | copy-start | bytes 2359300
  5.1 1.1 %copy-start.4 = (bf16[384,1024]{1,0:T(8,128)(2,1)S(1)}, bf16[384,1024]{1,0:T(8,128)(2,1)}, u32[]{:S(2)}) copy-start(bf16[384,1024]{1,0:T(8,128)(2,1)} %k_ref.1) | copy-start | bytes 2359300
  6.3 50.9 %copy-start.1 = (bf16[384,1024]{1,0:T(8,128)(2,1)S(1)}, bf16[384,1024]{1,0:T(8,128)(2,1)}, u32[]{:S(2)}) copy-start(bf16[384,1024]{1,0:T(8,128)(2,1)} %q_ref.3) | copy-start | bytes 2359300
  6.3 50.9 %copy-start.3 = (bf16[384,1024]{1,0:T(8,128)(2,1)S(1)}, bf16[384,1024]{1,0:T(8,128)(2,1)}, u32[]{:S(2)}) copy-start(bf16[384,1024]{1,0:T(8,128)(2,1)} %v_ref.3) | copy-start | bytes 2359300
  6.3 50.9 %copy-start.6 = (f32[1024]{0:T(1024)S(1)}, f32[1024]{0:T(1024)}, u32[]{:S(2)}) copy-start(f32[1024]{0:T(1024)} %param.10) | copy-start | bytes 12292
  11.3 12.9 %collective-permute-start = (bf16[3,8,128,128]{3,2,1,0:T(8,128)(2,1)S(1)}, bf16[3,8,128,128]{3,2,1,0:T(8,128)(2,1)S(1)}, u32[]{:S(2)}, u32[]{:S(2)}) collective-permute-start(bf16[3,8,128,128]{3,2,1,0:T(8,128)(2,1)S(1)} %get-tuple-element.8.own_ref), channel_id=1, source_target_pairs={{0,1},{1,0},{2,3},{3,2},{4,5},{5,4},{6,7},{7,6},{8,9},{9,8},{10,11... | collective-permute-start | bytes 2359304 | tf_op jit(solution)/shard_map/ppermute | solution.py:163
  12.0 11.3 %collective-permute-start.4 = (bf16[1024,128]{1,0:T(8,128)(2,1)S(1)}, bf16[1024,128]{1,0:T(8,128)(2,1)S(1)}, u32[]{:S(2)}, u32[]{:S(2)}) collective-permute-start(bf16[1024,128]{1,0:T(8,128)(2,1)S(1)} %copy-done.5), channel_id=1, source_target_pairs={{0,4},{1,5},{2,6},{3,7},{4,0},{5,1},{6,2},{7,3},{8,12},{9,13},{10,... | collective-permute-start | bytes 786440 | tf_op jit(solution)/shard_map/ppermute | solution.py:138
  13.3 12.9 %collective-permute-start.6 = (bf16[1024,128]{1,0:T(8,128)(2,1)S(1)}, bf16[1024,128]{1,0:T(8,128)(2,1)S(1)}, u32[]{:S(2)}, u32[]{:S(2)}) collective-permute-start(bf16[1024,128]{1,0:T(8,128)(2,1)S(1)} %copy-done.5), channel_id=1, source_target_pairs={{0,8},{1,9},{2,10},{3,11},{4,12},{5,13},{6,14},{7,15},{8,0},{9,1},... | collective-permute-start | bytes 786440 | tf_op jit(solution)/shard_map/ppermute | solution.py:138
  13.4 24.3 %collective-permute-start.8 = (bf16[1024,128]{1,0:T(8,128)(2,1)S(1)}, bf16[1024,128]{1,0:T(8,128)(2,1)S(1)}, u32[]{:S(2)}, u32[]{:S(2)}) collective-permute-start(bf16[1024,128]{1,0:T(8,128)(2,1)S(1)} %copy-done.5), channel_id=1, source_target_pairs={{0,12},{1,13},{2,14},{3,15},{4,8},{5,9},{6,10},{7,11},{8,4},{9,5},... | collective-permute-start | bytes 786440 | tf_op jit(solution)/shard_map/ppermute | solution.py:138
  14.7 24.2 %collective-permute-start.3 = (bf16[1024,128]{1,0:T(8,128)(2,1)S(1)}, bf16[1024,128]{1,0:T(8,128)(2,1)S(1)}, u32[]{:S(2)}, u32[]{:S(2)}) collective-permute-start(bf16[1024,128]{1,0:T(8,128)(2,1)S(1)} %copy-done.5), channel_id=1, source_target_pairs={{0,2},{1,3},{2,0},{3,1},{4,6},{5,7},{6,4},{7,5},{8,10},{9,11},{10,... | collective-permute-start | bytes 786440 | tf_op jit(solution)/shard_map/ppermute | solution.py:139
  23.4 15.8 %collective-permute-start.10 = (bf16[1024,128]{1,0:T(8,128)(2,1)S(1)}, bf16[1024,128]{1,0:T(8,128)(2,1)S(1)}, u32[]{:S(2)}, u32[]{:S(2)}) collective-permute-start(bf16[1024,128]{1,0:T(8,128)(2,1)S(1)} %copy-done.5), channel_id=1, source_target_pairs={{0,1},{1,0},{2,3},{3,2},{4,5},{5,4},{6,7},{7,6},{8,9},{9,8},{10,11... | collective-permute-start | bytes 786440 | tf_op jit(solution)/shard_map/ppermute | solution.py:144
  24.2 17.0 %collective-permute-start.5 = (bf16[1024,128]{1,0:T(8,128)(2,1)S(1)}, bf16[1024,128]{1,0:T(8,128)(2,1)S(1)}, u32[]{:S(2)}, u32[]{:S(2)}) collective-permute-start(bf16[1024,128]{1,0:T(8,128)(2,1)S(1)} %collective-permute-done.4.refs_2_), channel_id=1, source_target_pairs={{0,2},{1,3},{2,0},{3,1},{4,6},{5,7},{6,4},{7,5},{8,10},{9,11},{10,... | collective-permute-start | bytes 786440 | tf_op jit(solution)/shard_map/ppermute | solution.py:142
  26.2 18.1 %collective-permute-start.1 = (bf16[2,4,128,128]{3,2,1,0:T(8,128)(2,1)S(1)}, bf16[2,4,128,128]{3,2,1,0:T(8,128)(2,1)S(1)}, u32[]{:S(2)}, u32[]{:S(2)}) collective-permute-start(bf16[2,4,128,128]{3,2,1,0:T(8,128)(2,1)S(1)} %chip_state.1), channel_id=1, source_target_pairs={{0,2},{1,3},{2,4},{3,5},{4,6},{5,7},{6,8},{7,9},{8,10},{9,11},{10,... | collective-permute-start | bytes 786440 | tf_op jit(solution)/shard_map/ppermute | solution.py:171
  37.7 12.9 %collective-permute-start.7 = (bf16[1024,128]{1,0:T(8,128)(2,1)S(1)}, bf16[1024,128]{1,0:T(8,128)(2,1)S(1)}, u32[]{:S(2)}, u32[]{:S(2)}) collective-permute-start(bf16[1024,128]{1,0:T(8,128)(2,1)S(1)} %collective-permute-done.6.refs_4_), channel_id=1, source_target_pairs={{0,2},{1,3},{2,0},{3,1},{4,6},{5,7},{6,4},{7,5},{8,10},{9,11},{10,... | collective-permute-start | bytes 786440 | tf_op jit(solution)/shard_map/ppermute | solution.py:142
  38.9 17.3 %collective-permute-start.9 = (bf16[1024,128]{1,0:T(8,128)(2,1)S(1)}, bf16[1024,128]{1,0:T(8,128)(2,1)S(1)}, u32[]{:S(2)}, u32[]{:S(2)}) collective-permute-start(bf16[1024,128]{1,0:T(8,128)(2,1)S(1)} %collective-permute-done.8.refs_6_), channel_id=1, source_target_pairs={{0,2},{1,3},{2,0},{3,1},{4,6},{5,7},{6,4},{7,5},{8,10},{9,11},{10,... | collective-permute-start | bytes 786440 | tf_op jit(solution)/shard_map/ppermute | solution.py:142
  39.1 17.5 %collective-permute-start.12 = (bf16[1024,128]{1,0:T(8,128)(2,1)S(1)}, bf16[1024,128]{1,0:T(8,128)(2,1)S(1)}, u32[]{:S(2)}, u32[]{:S(2)}) collective-permute-start(bf16[1024,128]{1,0:T(8,128)(2,1)S(1)} %collective-permute-done.4.refs_2_), channel_id=1, source_target_pairs={{0,1},{1,0},{2,3},{3,2},{4,5},{5,4},{6,7},{7,6},{8,9},{9,8},{10,11... | collective-permute-start | bytes 786440 | tf_op jit(solution)/shard_map/ppermute | solution.py:144
  41.2 15.5 %collective-permute-start.14 = (bf16[1024,128]{1,0:T(8,128)(2,1)S(1)}, bf16[1024,128]{1,0:T(8,128)(2,1)S(1)}, u32[]{:S(2)}, u32[]{:S(2)}) collective-permute-start(bf16[1024,128]{1,0:T(8,128)(2,1)S(1)} %collective-permute-done.6.refs_4_), channel_id=1, source_target_pairs={{0,1},{1,0},{2,3},{3,2},{4,5},{5,4},{6,7},{7,6},{8,9},{9,8},{10,11... | collective-permute-start | bytes 786440 | tf_op jit(solution)/shard_map/ppermute | solution.py:144
  44.3 12.9 %collective-permute-start.2 = (bf16[2,4,128,128]{3,2,1,0:T(8,128)(2,1)S(1)}, bf16[2,4,128,128]{3,2,1,0:T(8,128)(2,1)S(1)}, u32[]{:S(2)}, u32[]{:S(2)}) collective-permute-start(bf16[2,4,128,128]{3,2,1,0:T(8,128)(2,1)S(1)} %collective-permute-done.1.same_ref), channel_id=1, source_target_pairs={{0,1},{1,0},{2,3},{3,2},{4,5},{5,4},{6,7},{7,6},{8,9},{9,8},{10,11... | collective-permute-start | bytes 786440 | tf_op jit(solution)/shard_map/ppermute | solution.py:172
  50.5 12.0 %collective-permute-start.16 = (bf16[1024,128]{1,0:T(8,128)(2,1)S(1)}, bf16[1024,128]{1,0:T(8,128)(2,1)S(1)}, u32[]{:S(2)}, u32[]{:S(2)}) collective-permute-start(bf16[1024,128]{1,0:T(8,128)(2,1)S(1)} %collective-permute-done.8.refs_6_), channel_id=1, source_target_pairs={{0,1},{1,0},{2,3},{3,2},{4,5},{5,4},{6,7},{7,6},{8,9},{9,8},{10,11... | collective-permute-start | bytes 786440 | tf_op jit(solution)/shard_map/ppermute | solution.py:144
  56.1 6.4 %collective-permute-start.11 = (bf16[1024,128]{1,0:T(8,128)(2,1)S(1)}, bf16[1024,128]{1,0:T(8,128)(2,1)S(1)}, u32[]{:S(2)}, u32[]{:S(2)}) collective-permute-start(bf16[1024,128]{1,0:T(8,128)(2,1)S(1)} %collective-permute-done.3.refs_1_), channel_id=1, source_target_pairs={{0,1},{1,0},{2,3},{3,2},{4,5},{5,4},{6,7},{7,6},{8,9},{9,8},{10,11... | collective-permute-start | bytes 786440 | tf_op jit(solution)/shard_map/ppermute | solution.py:144
  56.6 5.9 %collective-permute-start.13 = (bf16[1024,128]{1,0:T(8,128)(2,1)S(1)}, bf16[1024,128]{1,0:T(8,128)(2,1)S(1)}, u32[]{:S(2)}, u32[]{:S(2)}) collective-permute-start(bf16[1024,128]{1,0:T(8,128)(2,1)S(1)} %collective-permute-done.5.refs_3_), channel_id=1, source_target_pairs={{0,1},{1,0},{2,3},{3,2},{4,5},{5,4},{6,7},{7,6},{8,9},{9,8},{10,11... | collective-permute-start | bytes 786440 | tf_op jit(solution)/shard_map/ppermute | solution.py:144
  56.6 5.9 %collective-permute-start.15 = (bf16[1024,128]{1,0:T(8,128)(2,1)S(1)}, bf16[1024,128]{1,0:T(8,128)(2,1)S(1)}, u32[]{:S(2)}, u32[]{:S(2)}) collective-permute-start(bf16[1024,128]{1,0:T(8,128)(2,1)S(1)} %collective-permute-done.7.refs_5_), channel_id=1, source_target_pairs={{0,1},{1,0},{2,3},{3,2},{4,5},{5,4},{6,7},{7,6},{8,9},{9,8},{10,11... | collective-permute-start | bytes 786440 | tf_op jit(solution)/shard_map/ppermute | solution.py:144
  57.1 5.4 %collective-permute-start.17 = (bf16[1024,128]{1,0:T(8,128)(2,1)S(1)}, bf16[1024,128]{1,0:T(8,128)(2,1)S(1)}, u32[]{:S(2)}, u32[]{:S(2)}) collective-permute-start(bf16[1024,128]{1,0:T(8,128)(2,1)S(1)} %collective-permute-done.9.refs_7_), channel_id=1, source_target_pairs={{0,1},{1,0},{2,3},{3,2},{4,5},{5,4},{6,7},{7,6},{8,9},{9,8},{10,11... | collective-permute-start | bytes 786440 | tf_op jit(solution)/shard_map/ppermute | solution.py:144

commit v2 on v1

v2 whole, which is shorter than its diff:
```python
import functools

import jax
import jax.numpy as jnp
from jax import lax
from jax.experimental import pallas as pl
from jax.experimental.pallas import tpu as pltpu
from jax.sharding import PartitionSpec as P

HD = 128
EPS = 1e-05
BF = jnp.bfloat16
F32 = jnp.float32
MIB = 1024 * 1024


def dot(a, b, ca, cb):
    return lax.dot_general(a, b, (((ca,), (cb,)), ((), ())), preferred_element_type=F32)


def params(mib=48):
    return pltpu.CompilerParams(vmem_limit_bytes=mib * MIB)


def scalars(resets, blocks, length):
    index = lax.axis_index("ctx")
    core, chip = lax.rem(index, 2), lax.div(index, 2)
    pair = resets[chip] - chip * (2 * length)
    local = pair - core * length
    has = (local >= 0) & (local < length)
    cut = jnp.where(has, local, 0)
    has_second = pair >= length
    return index, core, chip, has, cut, has_second


def visible_mask(cut, length):
    row = lax.broadcasted_iota(jnp.int32, (length, length), 0)
    col = lax.broadcasted_iota(jnp.int32, (length, length), 1)
    return (col <= row) & ((row < cut) | (col >= cut))


def state_kernel(blocks, heads, step, resets, q_hbm, k_hbm, v_hbm, w_ref, *refs):
    steps = heads // step
    st_refs, (q_ref, k_ref, v_ref, sems) = refs[:steps], refs[steps:]
    length = q_ref.shape[0]
    width = step * HD
    copies = []
    for s in range(steps):
        at = slice(s * width, (s + 1) * width)
        for n, (src, dst) in enumerate(((q_hbm, q_ref), (k_hbm, k_ref), (v_hbm, v_ref))):
            copy = pltpu.make_async_copy(src.at[:, at], dst.at[:, at], sems.at[n, s])
            copy.start()
            copies.append(copy)
    _, _, _, has, cut, _ = scalars(resets, blocks, length)
    visible = visible_mask(cut, length)
    row = lax.broadcasted_iota(jnp.int32, (length, HD), 0)
    tail = (row >= cut) | jnp.logical_not(has)
    zero = jnp.zeros((), BF)
    for h in range(heads):
        if h % step == 0:
            for n in range(3):
                copies[(h // step) * 3 + n].wait()
        at = slice(h * HD, (h + 1) * HD)
        q, k, v = q_ref[:, at], k_ref[:, at], v_ref[:, at]
        scores = jnp.where(visible, dot(q, k, 1, 1), 0.0).astype(BF)
        w = dot(scores, k, 1, 0).astype(BF)
        w_ref[:, at] = w
        v_tail = jnp.where(tail, v, zero)
        k_tail = jnp.where(tail, k, zero)
        st_refs[h // step][0, h % step] = dot(k_tail, k, 0, 0).astype(BF)
        st_refs[h // step][1, h % step] = dot(q, v_tail, 0, 0).astype(BF)
        st_refs[h // step][2, h % step] = dot(w, v_tail, 0, 0).astype(BF)


def chip_kernel(blocks, length, half, step, resets, *refs):
    _, core, _, _, _, has_second = scalars(resets, blocks, length)
    groups = 2 * half // step
    own_refs, other_refs, out_ref = refs[:groups], refs[groups : 2 * groups], refs[-2:]
    first = core == 0
    keep = jnp.logical_not(has_second)
    for j in range(half):
        low, high = j // step, (j + half) // step

        def part(refs, n):
            return jnp.where(first, refs[low][n, j % step], refs[high][n, j % step]).astype(F32)

        own = [part(own_refs, n) for n in range(3)]
        oth = [part(other_refs, n) for n in range(3)]
        s0, h0 = jnp.where(first, own[0], oth[0]), jnp.where(first, own[2], oth[2])
        s1, c1, h1 = (jnp.where(first, oth[n], own[n]) for n in range(3))
        through = dot(s0.astype(BF), c1.astype(BF), 1, 0)
        out_ref[0][j] = jnp.where(keep, s0 + s1, s1).astype(BF)
        out_ref[1][j] = jnp.where(keep, h0 + h1 + through, h1).astype(BF)


def output_kernel(blocks, heads, half, resets, q_ref, v_ref, w_ref, gain_ref, *refs):
    same_ref, swap_ref, other_refs, out_ref = refs[:2], refs[2:4], refs[4:-1], refs[-1]
    step = heads // len(other_refs)
    length = q_ref.shape[0]
    _, core, chip, has, cut, has_second = scalars(resets, blocks, length)
    second = core == 1
    keep_chip = (chip > 0) & (jnp.logical_not(second) | has_second)
    visible = visible_mask(cut, length)
    row = lax.broadcasted_iota(jnp.int32, (length, HD), 0)
    is_open = (row < cut) | jnp.logical_not(has)
    for h in range(heads):
        at = slice(h * HD, (h + 1) * HD)
        place = h % half
        mine = core == h // half
        s_chip = jnp.where(mine, same_ref[0][place], swap_ref[0][place]).astype(F32)
        h_chip = jnp.where(mine, same_ref[1][place], swap_ref[1][place]).astype(F32)
        s_chip = jnp.where(keep_chip, s_chip, 0.0)
        h_chip = jnp.where(keep_chip, h_chip, 0.0)
        s_in, c_in, h_in = (other_refs[h // step][n, h % step].astype(F32) for n in range(3))
        through = dot(s_chip.astype(BF), c_in.astype(BF), 1, 0)
        s_prev = jnp.where(second, s_chip + s_in, s_chip).astype(BF)
        h_prev = jnp.where(second, h_chip + h_in + through, h_chip).astype(BF)
        q, v = q_ref[:, at], v_ref[:, at]
        w = w_ref[:, at].astype(F32) + jnp.where(is_open, dot(q, s_prev, 1, 0), 0.0)
        scores = jnp.where(visible, dot(q, w.astype(BF), 1, 1), 0.0).astype(BF)
        summed = dot(scores, v, 1, 0) + jnp.where(is_open, dot(q, h_prev, 1, 0), 0.0)
        inverse = lax.rsqrt(jnp.mean(summed * summed, axis=1, keepdims=True) + EPS)
        out_ref[:, at] = (summed * inverse * gain_ref[:, at]).astype(BF)


def project_kernel(masks, hidden_ref, *refs):
    pairs = len(masks)
    same, other, (out_hbm, buffer, sems) = refs[:pairs], refs[pairs : 2 * pairs], refs[-3:]
    index = lax.axis_index("ctx")
    first = lax.rem(index, 2) == 0
    cols = 2 * same[0].shape[1]
    copies = []
    for n, mask in enumerate(masks):
        a, b = same[n][...], other[n][...]
        both = jnp.concatenate([jnp.where(first, a, b), jnp.where(first, b, a)], axis=1)
        buffer[n] = dot(hidden_ref[...], both, 1, 0).astype(BF)
        at = pl.multiple_of(lax.div(index ^ mask, 2) * cols, cols)
        copy = pltpu.make_async_copy(buffer.at[n], out_hbm.at[:, pl.ds(at, cols)], sems.at[n])
        copy.start()
        copies.append(copy)
    for copy in copies:
        copy.wait()


def project(hidden, masks, same, other, shape, before=None):
    pairs = len(masks)
    extra = [] if before is None else [before]
    length, cols = hidden.shape[0], 2 * same[0].shape[1]
    return pl.pallas_call(
        functools.partial(project_kernel, masks),
        in_specs=[pl.BlockSpec(memory_space=pltpu.VMEM)] * (1 + 2 * pairs) + [anywhere()] * len(extra),
        out_specs=anywhere(),
        out_shape=shape,
        input_output_aliases={} if before is None else {1 + 2 * pairs: 0},
        scratch_shapes=[pltpu.VMEM((pairs, length, cols), BF), pltpu.SemaphoreType.DMA((pairs,))],
        compiler_params=params(),
        name="project",
    )(hidden, *same, *other, *extra)


def anywhere():
    return pl.BlockSpec(memory_space=pltpu.HBM)


def smem():
    return pl.BlockSpec(memory_space=pltpu.SMEM)


def swap_by(mask, n):
    return [(i, i ^ mask) for i in range(n)]


def on_device(blocks, queries, keys, values, reset_points, norm_gain, out_weight):
    length, width = queries.shape
    heads = width // HD
    half = heads // 2
    n_ctx = blocks
    per_span = n_ctx // reset_points.shape[0]
    assert per_span == 2 and heads % 2 == 0
    small = n_ctx == 16 and out_weight.shape[1] == HD

    def swap(piece, mask, *after):
        if after:
            piece, *_ = lax.optimization_barrier((piece, *after))
        return lax.ppermute(piece, "ctx", swap_by(mask, n_ctx))

    if small:
        pieces = {0: out_weight, 2: swap(out_weight, 2), 4: swap(out_weight, 4), 8: swap(out_weight, 8)}

    step_heads = 2
    steps = heads // step_heads
    whole_vmem = pl.BlockSpec(memory_space=pltpu.VMEM)
    any_place = pl.BlockSpec(memory_space=pl.ANY)
    w, *state = pl.pallas_call(
        functools.partial(state_kernel, n_ctx, heads, step_heads),
        in_specs=[smem(), anywhere(), anywhere(), anywhere()],
        out_specs=[whole_vmem] * (1 + steps),
        out_shape=[jax.ShapeDtypeStruct((length, width), BF)]
        + [jax.ShapeDtypeStruct((3, step_heads, HD, HD), BF)] * steps,
        scratch_shapes=[pltpu.VMEM((length, width), BF)] * 3 + [pltpu.SemaphoreType.DMA((3, steps))],
        compiler_params=params(),
        name="block_state",
    )(reset_points, *(pltpu.with_memory_space_constraint(a, pltpu.HBM) for a in (queries, keys, values)))
    if small:
        *state_sent, _, _ = lax.optimization_barrier((*state, pieces[2], pieces[4]))
    else:
        state_sent = state
    state_other = [swap(part, 1) for part in state_sent]
    waited = []
    if small:
        pieces[6] = swap(pieces[4], 2, w)
        waited = [pieces[6], pieces[8]]
    chip_state = pl.pallas_call(
        functools.partial(chip_kernel, n_ctx, length, half, step_heads),
        in_specs=[smem()] + [whole_vmem] * (2 * steps) + [any_place] * len(waited),
        out_shape=[jax.ShapeDtypeStruct((half, HD, HD), BF)] * 2,
        compiler_params=params(),
        name="chip_state",
    )(reset_points, *state, *state_other, *waited)
    before = [lax.ppermute(part, "ctx", [(i, i + 2) for i in range(n_ctx - 2)]) for part in chip_state]
    if small:
        pieces[12] = swap(out_weight, 12, pieces[4])
        for m in (8, 12):
            pieces[m + 2] = swap(pieces[m], 2)
        others = {m: swap(pieces[m], 1) for m in (0, 2, 4, 6, 8, 10, 12)}
        before_swap = [swap(part, 1, pieces[12], pieces[10]) for part in before]
    else:
        before_swap = [swap(part, 1) for part in before]
    hidden = pl.pallas_call(
        functools.partial(output_kernel, n_ctx, heads, half),
        in_specs=[smem()] + [whole_vmem] * (8 + steps),
        out_shape=jax.ShapeDtypeStruct((length, width), BF),
        compiler_params=params(),
        name="block_output",
    )(reset_points, queries, values, w, norm_gain.reshape(1, width), *before, *before_swap, *state_other)
    if not small:
        whole = lax.all_gather(out_weight, "ctx", axis=1, tiled=True)
        return jnp.dot(hidden, whole, preferred_element_type=F32).astype(BF)
    shape = jax.ShapeDtypeStruct((length, n_ctx * out_weight.shape[1]), BF)
    masks = (0, 2, 4, 6, 8, 10, 12)
    out = project(hidden, masks, [pieces[m] for m in masks], [others[m] for m in masks], shape)
    last = swap(pieces[14], 1, out)
    return project(hidden, (14,), [pieces[14]], [last], shape, out)


def solution(mesh):
    placed = (
        P(("groups", "ctx"), None),
        P(("groups", "ctx"), None),
        P(("groups", "ctx"), None),
        P("groups"),
        P(),
        P(None, "ctx"),
    )
    return jax.shard_map(
        functools.partial(on_device, mesh.shape["ctx"]),
        mesh=mesh,
        in_specs=placed,
        out_specs=P(("groups", "ctx"), None),
        check_vma=False,
    )
```

time: 66.5 us -> 48.2 us (0.72)
  the two profiles are of different devices: /device:TPU:17 before, /device:TPU:13 now
where the time goes in v2:
time: 48.2 us; the launch traced here: 48 us
  starting transfers between devices  25.4 us (53%)
  Pallas kernels  14.1 us (29%)
  waiting for transfers between devices  7.69 us (16%)
  local copies, waits for them, and re-layouts  0.68 us (1%)
    ppermute x21, starting transfers between devices, swap(): return lax.ppermute(piece, 'ctx', swap_by(mask, n_ctx))  19.7 us
    ppermute x2, starting transfers between devices, on_device(): lax.ppermute(part, 'ctx', [(i, i + 2) for i in range(n_ctx - 2)])  5.71 us
    pallas_call x1, Pallas kernels, on_device(): pl.pallas_call(functools.partial(state_kernel, n_ctx, heads, step_heads),...  5.65 us
    ppermute x21, waiting for transfers between devices, swap(): return lax.ppermute(piece, 'ctx', swap_by(mask, n_ctx))  4.95 us
    pallas_call x1, Pallas kernels, on_device(): pl.pallas_call(functools.partial(output_kernel, n_ctx, heads, half), in_s...  4.06 us
    pallas_call x2, Pallas kernels, project(): pl.pallas_call(functools.partial(project_kernel, masks), in_specs=[pl.Blo...  3.55 us
    ppermute x2, waiting for transfers between devices, on_device(): lax.ppermute(part, 'ctx', [(i, i + 2) for i in range(n_ctx - 2)])  2.74 us
  transfers between devices with their start and end apart: 23, of which 6 were waited for; matrix products, arithmetic and copies ran while one was open for 0% of the time, Pallas kernels for 27%

profile of v2, /device:TPU:13, one launch (start us, length us, event | category | flops | bytes accessed | tf_op | source)
XLA Modules:
  0.0 48.0 jit_solution(4882855508326976881)
XLA Ops:
  0.0 0.2 collective-permute-start.1
  0.2 1.2 %collective-permute-start = (bf16[1024,128]{1,0:T(8,128)(2,1)}, bf16[1024,128]{1,0:T(8,128)(2,1)S(1)}, u32[]{:S(2)}, u32[]{:S(2)}) collective-permute-start(bf16[1024,128]{1,0:T(8,128)(2,1)} %refs_0_.1), channel_id=1, source_target_pairs={{0,2},{1,3},{2,0},{3,1},{4,6},{5,7},{6,4},{7,5},{8,10},{9,11},{10,... | collective-permute-start | bytes 786440 | tf_op jit(solution)/shard_map/ppermute | solution.py:185
  1.4 2.3 %collective-permute-start.7 = (bf16[1024,128]{1,0:T(8,128)(2,1)}, bf16[1024,128]{1,0:T(8,128)(2,1)S(1)}, u32[]{:S(2)}, u32[]{:S(2)}) collective-permute-start(bf16[1024,128]{1,0:T(8,128)(2,1)} %refs_0_.1), channel_id=1, source_target_pairs={{0,8},{1,9},{2,10},{3,11},{4,12},{5,13},{6,14},{7,15},{8,0},{9,1},... | collective-permute-start | bytes 786440 | tf_op jit(solution)/shard_map/ppermute | solution.py:185
  3.7 0.7 %copy-done.3 = s32[8]{0:T(128)S(1)} copy-done((s32[8]{0:T(128)S(1)}, s32[8]{0:T(128)}, u32[]{:S(2)}) %copy-start.3) | copy-done | bytes 56
  4.3 5.7 %block_state.1 = (bf16[384,1024]{1,0:T(8,128)(2,1)S(1)}, bf16[3,2,128,128]{3,2,1,0:T(8,128)(2,1)S(1)}, bf16[3,2,128,128]{3,2,1,0:T(8,128)(2,1)S(1)}, bf16[3,2,12...) custom-call(s32[8]{0:T(128)S(1)} %copy-done.3, bf16[384,1024]{1,0:T(8,128)(2,1)} %q_ref.1, bf16[384,1024]{1,0:T(8,128)(2,1)} %k_hbm.1, ...), custom_call_target="tpu_custom_call" | custom-call | tf_op jit(solution)/shard_map/block_state/pallas_call | solution.py:194
  10.1 1.6 %collective-permute-start.2 = (bf16[3,2,128,128]{3,2,1,0:T(8,128)(2,1)S(1)}, bf16[3,2,128,128]{3,2,1,0:T(8,128)(2,1)S(1)}, u32[]{:S(2)}, u32[]{:S(2)}) collective-permute-start(bf16[3,2,128,128]{3,2,1,0:T(8,128)(2,1)S(1)} %get-tuple-element.26.refs_0_), channel_id=1, source_target_pairs={{0,1},{1,0},{2,3},{3,2},{4,5},{5,4},{6,7},{7,6},{8,9},{9,8},{10,11... | collective-permute-start | bytes 589832 | tf_op jit(solution)/shard_map/ppermute | solution.py:185
  11.6 0.1 collective-permute-start.3
  11.7 1.7 %collective-permute-start.6 = (bf16[1024,128]{1,0:T(8,128)(2,1)S(1)}, bf16[1024,128]{1,0:T(8,128)(2,1)S(1)}, u32[]{:S(2)}, u32[]{:S(2)}) collective-permute-start(bf16[1024,128]{1,0:T(8,128)(2,1)S(1)} %collective-permute-done.1.refs_2_), channel_id=1, source_target_pairs={{0,2},{1,3},{2,0},{3,1},{4,6},{5,7},{6,4},{7,5},{8,10},{9,11},{10,... | collective-permute-start | bytes 786440 | tf_op jit(solution)/shard_map/ppermute | solution.py:185
  13.5 1.3 %collective-permute-start.10 = (bf16[1024,128]{1,0:T(8,128)(2,1)S(1)}, bf16[1024,128]{1,0:T(8,128)(2,1)S(1)}, u32[]{:S(2)}, u32[]{:S(2)}) collective-permute-start(bf16[1024,128]{1,0:T(8,128)(2,1)S(1)} %copy-done.2), channel_id=1, source_target_pairs={{0,12},{1,13},{2,14},{3,15},{4,8},{5,9},{6,10},{7,11},{8,4},{9,5},... | collective-permute-start | bytes 786440 | tf_op jit(solution)/shard_map/ppermute | solution.py:185
  14.8 0.5 %collective-permute-start.11 = (bf16[1024,128]{1,0:T(8,128)(2,1)S(1)}, bf16[1024,128]{1,0:T(8,128)(2,1)S(1)}, u32[]{:S(2)}, u32[]{:S(2)}) collective-permute-start(bf16[1024,128]{1,0:T(8,128)(2,1)S(1)} %collective-permute-done.7.refs_9_.refs_4_), channel_id=1, source_target_pairs={{0,2},{1,3},{2,0},{3,1},{4,6},{5,7},{6,4},{7,5},{8,10},{9,11},{10,... | collective-permute-start | bytes 786440 | tf_op jit(solution)/shard_map/ppermute | solution.py:185
  15.3 2.0 %collective-permute-start.4 = (bf16[3,2,128,128]{3,2,1,0:T(8,128)(2,1)S(1)}, bf16[3,2,128,128]{3,2,1,0:T(8,128)(2,1)S(1)}, u32[]{:S(2)}, u32[]{:S(2)}) collective-permute-start(bf16[3,2,128,128]{3,2,1,0:T(8,128)(2,1)S(1)} %get-tuple-element.28.refs_2_), channel_id=1, source_target_pairs={{0,1},{1,0},{2,3},{3,2},{4,5},{5,4},{6,7},{7,6},{8,9},{9,8},{10,11... | collective-permute-start | bytes 589832 | tf_op jit(solution)/shard_map/ppermute | solution.py:185
  17.3 0.1 collective-permute-start.5
  17.3 1.0 %collective-permute-done.4.refs_6_ = bf16[3,2,128,128]{3,2,1,0:T(8,128)(2,1)S(1)} collective-permute-done((bf16[3,2,128,128]{3,2,1,0:T(8,128)(2,1)S(1)}, bf16[3,2,128,128]{3,2,1,0:T(8,128)(2,1)S(1)}, u32[]{:S(2)}, u32[]{:S(2)}) %collective-permute-start.4) | collective-permute-done | bytes 196640 | tf_op jit(solution)/shard_map/ppermute | solution.py:185
  18.3 0.4 collective-permute-start.15
  18.7 1.0 %collective-permute-done.6.refs_8_.refs_3_ = bf16[1024,128]{1,0:T(8,128)(2,1)S(1)} collective-permute-done((bf16[1024,128]{1,0:T(8,128)(2,1)S(1)}, bf16[1024,128]{1,0:T(8,128)(2,1)S(1)}, u32[]{:S(2)}, u32[]{:S(2)}) %collective-permute-start.6) | collective-permute-done | bytes 262176 | tf_op jit(solution)/shard_map/ppermute | solution.py:185
  19.7 0.8 %chip_state.1 = (bf16[4,128,128]{2,1,0:T(8,128)(2,1)S(1)}, bf16[4,128,128]{2,1,0:T(8,128)(2,1)S(1)}) custom-call(s32[8]{0:T(128)S(1)} %copy-done.3, bf16[3,2,128,128]{3,2,1,0:T(8,128)(2,1)S(1)} %get-tuple-element.26.refs_0_, bf16[3,2,128,128]{3,2,1,0:T(8,128)(2,1)S(1)} %get-tuple-element.27.refs_1_, bf16[3,2,128,128]{3,2,1,0:T(8,128)(2,1)S(1)} %get-tuple-element.28.refs_2_, ...), custom_call_target="tpu_custom_call" | custom-call | tf_op jit(solution)/shard_map/chip_state/pallas_call | solution.py:213
  20.5 3.1 %collective-permute-start.9 = (bf16[4,128,128]{2,1,0:T(8,128)(2,1)S(1)}, bf16[4,128,128]{2,1,0:T(8,128)(2,1)S(1)}, u32[]{:S(2)}, u32[]{:S(2)}) collective-permute-start(bf16[4,128,128]{2,1,0:T(8,128)(2,1)S(1)} %get-tuple-element.32), channel_id=1, source_target_pairs={{0,2},{1,3},{2,4},{3,5},{4,6},{5,7},{6,8},{7,9},{8,10},{9,11},{10,... | collective-permute-start | bytes 393224 | tf_op jit(solution)/shard_map/ppermute | solution.py:220
  23.5 2.7 %collective-permute-start.17 = (bf16[1024,128]{1,0:T(8,128)(2,1)S(1)}, bf16[1024,128]{1,0:T(8,128)(2,1)S(1)}, u32[]{:S(2)}, u32[]{:S(2)}) collective-permute-start(bf16[1024,128]{1,0:T(8,128)(2,1)S(1)} %collective-permute-done.1.refs_2_), channel_id=1, source_target_pairs={{0,1},{1,0},{2,3},{3,2},{4,5},{5,4},{6,7},{7,6},{8,9},{9,8},{10,11... | collective-permute-start | bytes 786440 | tf_op jit(solution)/shard_map/ppermute | solution.py:185
  26.2 0.8 %collective-permute-done.10.refs_6_ = bf16[1024,128]{1,0:T(8,128)(2,1)S(1)} collective-permute-done((bf16[1024,128]{1,0:T(8,128)(2,1)S(1)}, bf16[1024,128]{1,0:T(8,128)(2,1)S(1)}, u32[]{:S(2)}, u32[]{:S(2)}) %collective-permute-start.10) | collective-permute-done | bytes 262176 | tf_op jit(solution)/shard_map/ppermute | solution.py:185
  27.0 2.7 %collective-permute-start.8 = (bf16[4,128,128]{2,1,0:T(8,128)(2,1)S(1)}, bf16[4,128,128]{2,1,0:T(8,128)(2,1)S(1)}, u32[]{:S(2)}, u32[]{:S(2)}) collective-permute-start(bf16[4,128,128]{2,1,0:T(8,128)(2,1)S(1)} %get-tuple-element.31), channel_id=1, source_target_pairs={{0,2},{1,3},{2,4},{3,5},{4,6},{5,7},{6,8},{7,9},{8,10},{9,11},{10,... | collective-permute-start | bytes 393224 | tf_op jit(solution)/shard_map/ppermute | solution.py:220
  29.7 1.1 %collective-permute-start.19 = (bf16[1024,128]{1,0:T(8,128)(2,1)S(1)}, bf16[1024,128]{1,0:T(8,128)(2,1)S(1)}, u32[]{:S(2)}, u32[]{:S(2)}) collective-permute-start(bf16[1024,128]{1,0:T(8,128)(2,1)S(1)} %collective-permute-done.7.refs_9_.refs_4_), channel_id=1, source_target_pairs={{0,1},{1,0},{2,3},{3,2},{4,5},{5,4},{6,7},{7,6},{8,9},{9,8},{10,11... | collective-permute-start | bytes 786440 | tf_op jit(solution)/shard_map/ppermute | solution.py:185
  30.8 0.1 collective-permute-start.13
  30.9 2.7 %collective-permute-done.8.refs_0_ = bf16[4,128,128]{2,1,0:T(8,128)(2,1)S(1)} collective-permute-done((bf16[4,128,128]{2,1,0:T(8,128)(2,1)S(1)}, bf16[4,128,128]{2,1,0:T(8,128)(2,1)S(1)}, u32[]{:S(2)}, u32[]{:S(2)}) %collective-permute-start.8) | collective-permute-done | bytes 131104 | tf_op jit(solution)/shard_map/ppermute | solution.py:220
  33.6 2.4 %collective-permute-start.12 = (bf16[4,128,128]{2,1,0:T(8,128)(2,1)S(1)}, bf16[4,128,128]{2,1,0:T(8,128)(2,1)S(1)}, u32[]{:S(2)}, u32[]{:S(2)}) collective-permute-start(bf16[4,128,128]{2,1,0:T(8,128)(2,1)S(1)} %collective-permute-done.8.refs_0_), channel_id=1, source_target_pairs={{0,1},{1,0},{2,3},{3,2},{4,5},{5,4},{6,7},{7,6},{8,9},{9,8},{10,11... | collective-permute-start | bytes 393224 | tf_op jit(solution)/shard_map/ppermute | solution.py:185
  36.0 0.5 %collective-permute-start.18 = (bf16[1024,128]{1,0:T(8,128)(2,1)S(1)}, bf16[1024,128]{1,0:T(8,128)(2,1)S(1)}, u32[]{:S(2)}, u32[]{:S(2)}) collective-permute-start(bf16[1024,128]{1,0:T(8,128)(2,1)S(1)} %collective-permute-done.6.refs_8_.refs_3_), channel_id=1, source_target_pairs={{0,1},{1,0},{2,3},{3,2},{4,5},{5,4},{6,7},{7,6},{8,9},{9,8},{10,11... | collective-permute-start | bytes 786440 | tf_op jit(solution)/shard_map/ppermute | solution.py:185
  36.6 0.4 collective-permute-start.20
  37.1 4.1 %block_output.1.hidden_ref = bf16[384,1024]{1,0:T(8,128)(2,1)S(1)} custom-call(s32[8]{0:T(128)S(1)} %copy-done.3, bf16[384,1024]{1,0:T(8,128)(2,1)S(1)} %copy-done, bf16[384,1024]{1,0:T(8,128)(2,1)S(1)} %copy-done.1, bf16[384,1024]{1,0:T(8,128)(2,1)S(1)} %get-tuple-element.21.w_ref, f32[1,1024]{1,0:T(1,128)S(1)} %bitcast.1, ...), custom_call_target="tpu_custom_call" | custom-call | tf_op jit(solution)/shard_map/block_output/pallas_call | solution.py:229
  41.2 2.5 %project.2.refs_2_ = bf16[384,2048]{1,0:T(8,128)(2,1)} custom-call(bf16[384,1024]{1,0:T(8,128)(2,1)S(1)} %block_output.1.hidden_ref, bf16[1024,128]{1,0:T(8,128)(2,1)S(1)} %copy-done.2, bf16[1024,128]{1,0:T(8,128)(2,1)S(1)} %collective-permute-done.refs_1_, bf16[1024,128]{1,0:T(8,128)(2,1)S(1)} %collective-permute-done.1.refs_2_, ...), custom_call_target="tpu_custom_call" | custom-call | tf_op jit(solution)/shard_map/project/pallas_call | solution.py:149
  43.7 1.0 %collective-permute-done.14.refs_0_ = bf16[1024,128]{1,0:T(8,128)(2,1)S(1)} collective-permute-done((bf16[1024,128]{1,0:T(8,128)(2,1)S(1)}, bf16[1024,128]{1,0:T(8,128)(2,1)S(1)}, u32[]{:S(2)}, u32[]{:S(2)}) %collective-permute-start.14) | collective-permute-done | bytes 262176 | tf_op jit(solution)/shard_map/ppermute | solution.py:185
  44.6 1.1 %collective-permute-start.22 = (bf16[1024,128]{1,0:T(8,128)(2,1)S(1)}, bf16[1024,128]{1,0:T(8,128)(2,1)S(1)}, u32[]{:S(2)}, u32[]{:S(2)}) collective-permute-start(bf16[1024,128]{1,0:T(8,128)(2,1)S(1)} %collective-permute-done.14.refs_0_), channel_id=1, source_target_pairs={{0,1},{1,0},{2,3},{3,2},{4,5},{5,4},{6,7},{7,6},{8,9},{9,8},{10,11... | collective-permute-start | bytes 786440 | tf_op jit(solution)/shard_map/ppermute | solution.py:185
  45.8 1.2 %collective-permute-done.22.refs_1_ = bf16[1024,128]{1,0:T(8,128)(2,1)S(1)} collective-permute-done((bf16[1024,128]{1,0:T(8,128)(2,1)S(1)}, bf16[1024,128]{1,0:T(8,128)(2,1)S(1)}, u32[]{:S(2)}, u32[]{:S(2)}) %collective-permute-start.22) | collective-permute-done | bytes 262176 | tf_op jit(solution)/shard_map/ppermute | solution.py:185
  46.9 1.1 %project.3 = bf16[384,2048]{1,0:T(8,128)(2,1)} custom-call(bf16[384,1024]{1,0:T(8,128)(2,1)S(1)} %block_output.1.hidden_ref, bf16[1024,128]{1,0:T(8,128)(2,1)S(1)} %collective-permute-done.14.refs_0_, bf16[1024,128]{1,0:T(8,128)(2,1)S(1)} %collective-permute-done.22.refs_1_, bf16[384,2048]{1,0:T(8,128)(2,1)} %project.2.refs_2_), custom_call_target="tpu_custom_call", output_to_operand_aliasing={{}: (3, {})} | custom-call | tf_op jit(solution)/shard_map/project/pallas_call | solution.py:149
  (29 shorter events, 0.1 us)
Async XLA Ops:
  0.0 13.5 %copy-start.2 = (bf16[1024,128]{1,0:T(8,128)(2,1)S(1)}, bf16[1024,128]{1,0:T(8,128)(2,1)}, u32[]{:S(2)}) copy-start(bf16[1024,128]{1,0:T(8,128)(2,1)} %refs_0_.1) | copy-start | bytes 786436
  0.0 10.0 %collective-permute-start.1 = (bf16[1024,128]{1,0:T(8,128)(2,1)}, bf16[1024,128]{1,0:T(8,128)(2,1)S(1)}, u32[]{:S(2)}, u32[]{:S(2)}) collective-permute-start(bf16[1024,128]{1,0:T(8,128)(2,1)} %refs_0_.1), channel_id=1, source_target_pairs={{0,4},{1,5},{2,6},{3,7},{4,0},{5,1},{6,2},{7,3},{8,12},{9,13},{10,... | collective-permute-start | bytes 786440 | tf_op jit(solution)/shard_map/ppermute | solution.py:185
  0.2 9.9 %collective-permute-start = (bf16[1024,128]{1,0:T(8,128)(2,1)}, bf16[1024,128]{1,0:T(8,128)(2,1)S(1)}, u32[]{:S(2)}, u32[]{:S(2)}) collective-permute-start(bf16[1024,128]{1,0:T(8,128)(2,1)} %refs_0_.1), channel_id=1, source_target_pairs={{0,2},{1,3},{2,0},{3,1},{4,6},{5,7},{6,4},{7,5},{8,10},{9,11},{10,... | collective-permute-start | bytes 786440 | tf_op jit(solution)/shard_map/ppermute | solution.py:185
  1.4 13.4 %collective-permute-start.7 = (bf16[1024,128]{1,0:T(8,128)(2,1)}, bf16[1024,128]{1,0:T(8,128)(2,1)S(1)}, u32[]{:S(2)}, u32[]{:S(2)}) collective-permute-start(bf16[1024,128]{1,0:T(8,128)(2,1)} %refs_0_.1), channel_id=1, source_target_pairs={{0,8},{1,9},{2,10},{3,11},{4,12},{5,13},{6,14},{7,15},{8,0},{9,1},... | collective-permute-start | bytes 786440 | tf_op jit(solution)/shard_map/ppermute | solution.py:185
  3.7 0.7 %copy-start.3 = (s32[8]{0:T(128)S(1)}, s32[8]{0:T(128)}, u32[]{:S(2)}) copy-start(s32[8]{0:T(128)} %resets.5) | copy-start | bytes 100
  10.0 27.0 %copy-start = (bf16[384,1024]{1,0:T(8,128)(2,1)S(1)}, bf16[384,1024]{1,0:T(8,128)(2,1)}, u32[]{:S(2)}) copy-start(bf16[384,1024]{1,0:T(8,128)(2,1)} %q_ref.1) | copy-start | bytes 2359300
  10.0 27.0 %copy-start.1 = (bf16[384,1024]{1,0:T(8,128)(2,1)S(1)}, bf16[384,1024]{1,0:T(8,128)(2,1)}, u32[]{:S(2)}) copy-start(bf16[384,1024]{1,0:T(8,128)(2,1)} %v_ref.1) | copy-start | bytes 2359300
  10.0 27.0 %copy-start.4 = (f32[1024]{0:T(1024)S(1)}, f32[1024]{0:T(1024)}, u32[]{:S(2)}) copy-start(f32[1024]{0:T(1024)} %param.10) | copy-start | bytes 12292
  10.1 5.2 %collective-permute-start.2 = (bf16[3,2,128,128]{3,2,1,0:T(8,128)(2,1)S(1)}, bf16[3,2,128,128]{3,2,1,0:T(8,128)(2,1)S(1)}, u32[]{:S(2)}, u32[]{:S(2)}) collective-permute-start(bf16[3,2,128,128]{3,2,1,0:T(8,128)(2,1)S(1)} %get-tuple-element.26.refs_0_), channel_id=1, source_target_pairs={{0,1},{1,0},{2,3},{3,2},{4,5},{5,4},{6,7},{7,6},{8,9},{9,8},{10,11... | collective-permute-start | bytes 589832 | tf_op jit(solution)/shard_map/ppermute | solution.py:185
  11.6 5.6 %collective-permute-start.3 = (bf16[3,2,128,128]{3,2,1,0:T(8,128)(2,1)S(1)}, bf16[3,2,128,128]{3,2,1,0:T(8,128)(2,1)S(1)}, u32[]{:S(2)}, u32[]{:S(2)}) collective-permute-start(bf16[3,2,128,128]{3,2,1,0:T(8,128)(2,1)S(1)} %get-tuple-element.27.refs_1_), channel_id=1, source_target_pairs={{0,1},{1,0},{2,3},{3,2},{4,5},{5,4},{6,7},{7,6},{8,9},{9,8},{10,11... | collective-permute-start | bytes 589832 | tf_op jit(solution)/shard_map/ppermute | solution.py:185
  11.7 7.9 %collective-permute-start.6 = (bf16[1024,128]{1,0:T(8,128)(2,1)S(1)}, bf16[1024,128]{1,0:T(8,128)(2,1)S(1)}, u32[]{:S(2)}, u32[]{:S(2)}) collective-permute-start(bf16[1024,128]{1,0:T(8,128)(2,1)S(1)} %collective-permute-done.1.refs_2_), channel_id=1, source_target_pairs={{0,2},{1,3},{2,0},{3,1},{4,6},{5,7},{6,4},{7,5},{8,10},{9,11},{10,... | collective-permute-start | bytes 786440 | tf_op jit(solution)/shard_map/ppermute | solution.py:185
  13.5 13.6 %collective-permute-start.10 = (bf16[1024,128]{1,0:T(8,128)(2,1)S(1)}, bf16[1024,128]{1,0:T(8,128)(2,1)S(1)}, u32[]{:S(2)}, u32[]{:S(2)}) collective-permute-start(bf16[1024,128]{1,0:T(8,128)(2,1)S(1)} %copy-done.2), channel_id=1, source_target_pairs={{0,12},{1,13},{2,14},{3,15},{4,8},{5,9},{6,10},{7,11},{8,4},{9,5},... | collective-permute-start | bytes 786440 | tf_op jit(solution)/shard_map/ppermute | solution.py:185
  14.8 14.9 %collective-permute-start.11 = (bf16[1024,128]{1,0:T(8,128)(2,1)S(1)}, bf16[1024,128]{1,0:T(8,128)(2,1)S(1)}, u32[]{:S(2)}, u32[]{:S(2)}) collective-permute-start(bf16[1024,128]{1,0:T(8,128)(2,1)S(1)} %collective-permute-done.7.refs_9_.refs_4_), channel_id=1, source_target_pairs={{0,2},{1,3},{2,0},{3,1},{4,6},{5,7},{6,4},{7,5},{8,10},{9,11},{10,... | collective-permute-start | bytes 786440 | tf_op jit(solution)/shard_map/ppermute | solution.py:185
  15.3 3.1 %collective-permute-start.4 = (bf16[3,2,128,128]{3,2,1,0:T(8,128)(2,1)S(1)}, bf16[3,2,128,128]{3,2,1,0:T(8,128)(2,1)S(1)}, u32[]{:S(2)}, u32[]{:S(2)}) collective-permute-start(bf16[3,2,128,128]{3,2,1,0:T(8,128)(2,1)S(1)} %get-tuple-element.28.refs_2_), channel_id=1, source_target_pairs={{0,1},{1,0},{2,3},{3,2},{4,5},{5,4},{6,7},{7,6},{8,9},{9,8},{10,11... | collective-permute-start | bytes 589832 | tf_op jit(solution)/shard_map/ppermute | solution.py:185
  17.3 1.4 %collective-permute-start.5 = (bf16[3,2,128,128]{3,2,1,0:T(8,128)(2,1)S(1)}, bf16[3,2,128,128]{3,2,1,0:T(8,128)(2,1)S(1)}, u32[]{:S(2)}, u32[]{:S(2)}) collective-permute-start(bf16[3,2,128,128]{3,2,1,0:T(8,128)(2,1)S(1)} %get-tuple-element.29.refs_3_), channel_id=1, source_target_pairs={{0,1},{1,0},{2,3},{3,2},{4,5},{5,4},{6,7},{7,6},{8,9},{9,8},{10,11... | collective-permute-start | bytes 589832 | tf_op jit(solution)/shard_map/ppermute | solution.py:185
  18.3 17.7 %collective-permute-start.15 = (bf16[1024,128]{1,0:T(8,128)(2,1)S(1)}, bf16[1024,128]{1,0:T(8,128)(2,1)S(1)}, u32[]{:S(2)}, u32[]{:S(2)}) collective-permute-start(bf16[1024,128]{1,0:T(8,128)(2,1)S(1)} %copy-done.2), channel_id=1, source_target_pairs={{0,1},{1,0},{2,3},{3,2},{4,5},{5,4},{6,7},{7,6},{8,9},{9,8},{10,11... | collective-permute-start | bytes 786440 | tf_op jit(solution)/shard_map/ppermute | solution.py:185
  20.5 10.3 %collective-permute-start.9 = (bf16[4,128,128]{2,1,0:T(8,128)(2,1)S(1)}, bf16[4,128,128]{2,1,0:T(8,128)(2,1)S(1)}, u32[]{:S(2)}, u32[]{:S(2)}) collective-permute-start(bf16[4,128,128]{2,1,0:T(8,128)(2,1)S(1)} %get-tuple-element.32), channel_id=1, source_target_pairs={{0,2},{1,3},{2,4},{3,5},{4,6},{5,7},{6,8},{7,9},{8,10},{9,11},{10,... | collective-permute-start | bytes 393224 | tf_op jit(solution)/shard_map/ppermute | solution.py:220
  23.5 12.5 %collective-permute-start.17 = (bf16[1024,128]{1,0:T(8,128)(2,1)S(1)}, bf16[1024,128]{1,0:T(8,128)(2,1)S(1)}, u32[]{:S(2)}, u32[]{:S(2)}) collective-permute-start(bf16[1024,128]{1,0:T(8,128)(2,1)S(1)} %collective-permute-done.1.refs_2_), channel_id=1, source_target_pairs={{0,1},{1,0},{2,3},{3,2},{4,5},{5,4},{6,7},{7,6},{8,9},{9,8},{10,11... | collective-permute-start | bytes 786440 | tf_op jit(solution)/shard_map/ppermute | solution.py:185
  27.0 6.6 %collective-permute-start.8 = (bf16[4,128,128]{2,1,0:T(8,128)(2,1)S(1)}, bf16[4,128,128]{2,1,0:T(8,128)(2,1)S(1)}, u32[]{:S(2)}, u32[]{:S(2)}) collective-permute-start(bf16[4,128,128]{2,1,0:T(8,128)(2,1)S(1)} %get-tuple-element.31), channel_id=1, source_target_pairs={{0,2},{1,3},{2,4},{3,5},{4,6},{5,7},{6,8},{7,9},{8,10},{9,11},{10,... | collective-permute-start | bytes 393224 | tf_op jit(solution)/shard_map/ppermute | solution.py:220
  29.7 6.8 %collective-permute-start.19 = (bf16[1024,128]{1,0:T(8,128)(2,1)S(1)}, bf16[1024,128]{1,0:T(8,128)(2,1)S(1)}, u32[]{:S(2)}, u32[]{:S(2)}) collective-permute-start(bf16[1024,128]{1,0:T(8,128)(2,1)S(1)} %collective-permute-done.7.refs_9_.refs_4_), channel_id=1, source_target_pairs={{0,1},{1,0},{2,3},{3,2},{4,5},{5,4},{6,7},{7,6},{8,9},{9,8},{10,11... | collective-permute-start | bytes 786440 | tf_op jit(solution)/shard_map/ppermute | solution.py:185
  30.8 5.8 %collective-permute-start.13 = (bf16[4,128,128]{2,1,0:T(8,128)(2,1)S(1)}, bf16[4,128,128]{2,1,0:T(8,128)(2,1)S(1)}, u32[]{:S(2)}, u32[]{:S(2)}) collective-permute-start(bf16[4,128,128]{2,1,0:T(8,128)(2,1)S(1)} %collective-permute-done.9.refs_1_), channel_id=1, source_target_pairs={{0,1},{1,0},{2,3},{3,2},{4,5},{5,4},{6,7},{7,6},{8,9},{9,8},{10,11... | collective-permute-start | bytes 393224 | tf_op jit(solution)/shard_map/ppermute | solution.py:185
  33.6 3.4 %collective-permute-start.12 = (bf16[4,128,128]{2,1,0:T(8,128)(2,1)S(1)}, bf16[4,128,128]{2,1,0:T(8,128)(2,1)S(1)}, u32[]{:S(2)}, u32[]{:S(2)}) collective-permute-start(bf16[4,128,128]{2,1,0:T(8,128)(2,1)S(1)} %collective-permute-done.8.refs_0_), channel_id=1, source_target_pairs={{0,1},{1,0},{2,3},{3,2},{4,5},{5,4},{6,7},{7,6},{8,9},{9,8},{10,11... | collective-permute-start | bytes 393224 | tf_op jit(solution)/shard_map/ppermute | solution.py:185
  36.0 5.1 %collective-permute-start.16 = (bf16[1024,128]{1,0:T(8,128)(2,1)S(1)}, bf16[1024,128]{1,0:T(8,128)(2,1)S(1)}, u32[]{:S(2)}, u32[]{:S(2)}) collective-permute-start(bf16[1024,128]{1,0:T(8,128)(2,1)S(1)} %collective-permute-done.refs_1_), channel_id=1, source_target_pairs={{0,1},{1,0},{2,3},{3,2},{4,5},{5,4},{6,7},{7,6},{8,9},{9,8},{10,11... | collective-permute-start | bytes 786440 | tf_op jit(solution)/shard_map/ppermute | solution.py:185
  36.0 5.1 %collective-permute-start.18 = (bf16[1024,128]{1,0:T(8,128)(2,1)S(1)}, bf16[1024,128]{1,0:T(8,128)(2,1)S(1)}, u32[]{:S(2)}, u32[]{:S(2)}) collective-permute-start(bf16[1024,128]{1,0:T(8,128)(2,1)S(1)} %collective-permute-done.6.refs_8_.refs_3_), channel_id=1, source_target_pairs={{0,1},{1,0},{2,3},{3,2},{4,5},{5,4},{6,7},{7,6},{8,9},{9,8},{10,11... | collective-permute-start | bytes 786440 | tf_op jit(solution)/shard_map/ppermute | solution.py:185
  36.5 4.6 %collective-permute-start.21 = (bf16[1024,128]{1,0:T(8,128)(2,1)S(1)}, bf16[1024,128]{1,0:T(8,128)(2,1)S(1)}, u32[]{:S(2)}, u32[]{:S(2)}) collective-permute-start(bf16[1024,128]{1,0:T(8,128)(2,1)S(1)} %collective-permute-done.10.refs_6_), channel_id=1, source_target_pairs={{0,1},{1,0},{2,3},{3,2},{4,5},{5,4},{6,7},{7,6},{8,9},{9,8},{10,11... | collective-permute-start | bytes 786440 | tf_op jit(solution)/shard_map/ppermute | solution.py:185
  36.6 4.6 %collective-permute-start.20 = (bf16[1024,128]{1,0:T(8,128)(2,1)S(1)}, bf16[1024,128]{1,0:T(8,128)(2,1)S(1)}, u32[]{:S(2)}, u32[]{:S(2)}) collective-permute-start(bf16[1024,128]{1,0:T(8,128)(2,1)S(1)} %collective-permute-done.11.refs_5_), channel_id=1, source_target_pairs={{0,1},{1,0},{2,3},{3,2},{4,5},{5,4},{6,7},{7,6},{8,9},{9,8},{10,11... | collective-permute-start | bytes 786440 | tf_op jit(solution)/shard_map/ppermute | solution.py:185
  37.0 7.6 %collective-permute-start.14 = (bf16[1024,128]{1,0:T(8,128)(2,1)S(1)}, bf16[1024,128]{1,0:T(8,128)(2,1)S(1)}, u32[]{:S(2)}, u32[]{:S(2)}) collective-permute-start(bf16[1024,128]{1,0:T(8,128)(2,1)S(1)} %collective-permute-done.10.refs_6_), channel_id=1, source_target_pairs={{0,2},{1,3},{2,0},{3,1},{4,6},{5,7},{6,4},{7,5},{8,10},{9,11},{10,... | collective-permute-start | bytes 786440 | tf_op jit(solution)/shard_map/ppermute | solution.py:185
  44.6 2.3 %collective-permute-start.22 = (bf16[1024,128]{1,0:T(8,128)(2,1)S(1)}, bf16[1024,128]{1,0:T(8,128)(2,1)S(1)}, u32[]{:S(2)}, u32[]{:S(2)}) collective-permute-start(bf16[1024,128]{1,0:T(8,128)(2,1)S(1)} %collective-permute-done.14.refs_0_), channel_id=1, source_target_pairs={{0,1},{1,0},{2,3},{3,2},{4,5},{5,4},{6,7},{7,6},{8,9},{9,8},{10,11... | collective-permute-start | bytes 786440 | tf_op jit(solution)/shard_map/ppermute | solution.py:185

commit v3 on v2

--- a/solution.py
+++ b/solution.py
@@ -52,30 +52,41 @@
             copy.start()
             copies.append(copy)
     _, _, _, has, cut, _ = scalars(resets, blocks, length)
-    visible = visible_mask(cut, length)
+    visible = jnp.where(visible_mask(cut, length), 1.0, 0.0).astype(BF)
     row = lax.broadcasted_iota(jnp.int32, (length, HD), 0)
-    tail = (row >= cut) | jnp.logical_not(has)
-    zero = jnp.zeros((), BF)
+    tail = jnp.where((row >= cut) | jnp.logical_not(has), 1.0, 0.0).astype(BF)
+
+    def score(h):
+        at = slice(h * HD, (h + 1) * HD)
+        return dot(q_ref[:, at], k_ref[:, at], 1, 1).astype(BF) * visible
+
+    def finish(h, scores):
+        at = slice(h * HD, (h + 1) * HD)
+        q, k, v = q_ref[:, at], k_ref[:, at], v_ref[:, at]
+        w = dot(scores, k, 1, 0).astype(BF)
+        w_ref[:, at] = w
+        out = st_refs[h // step]
+        out[0, h % step] = dot((k * tail).T, k, 1, 0).astype(BF)
+        both = dot((v * tail).T, jnp.concatenate([q, w], axis=1), 1, 0).astype(BF)
+        out[1, h % step] = both[:, :HD]
+        out[2, h % step] = both[:, HD:]
+
+    ahead = None
     for h in range(heads):
         if h % step == 0:
             for n in range(3):
                 copies[(h // step) * 3 + n].wait()
-        at = slice(h * HD, (h + 1) * HD)
-        q, k, v = q_ref[:, at], k_ref[:, at], v_ref[:, at]
-        scores = jnp.where(visible, dot(q, k, 1, 1), 0.0).astype(BF)
-        w = dot(scores, k, 1, 0).astype(BF)
-        w_ref[:, at] = w
-        v_tail = jnp.where(tail, v, zero)
-        k_tail = jnp.where(tail, k, zero)
-        st_refs[h // step][0, h % step] = dot(k_tail, k, 0, 0).astype(BF)
-        st_refs[h // step][1, h % step] = dot(q, v_tail, 0, 0).astype(BF)
-        st_refs[h // step][2, h % step] = dot(w, v_tail, 0, 0).astype(BF)
+        scores = score(h)
+        if h > 0:
+            finish(h - 1, ahead)
+        ahead = scores
+    finish(heads - 1, ahead)
 
 
 def chip_kernel(blocks, length, half, step, resets, *refs):
     _, core, _, _, _, has_second = scalars(resets, blocks, length)
     groups = 2 * half // step
-    own_refs, other_refs, out_ref = refs[:groups], refs[groups : 2 * groups], refs[-2:]
+    own_refs, other_refs, out_ref = refs[:groups], refs[groups : 2 * groups], refs[-1]
     first = core == 0
     keep = jnp.logical_not(has_second)
     for j in range(half):
@@ -88,13 +99,13 @@
         oth = [part(other_refs, n) for n in range(3)]
         s0, h0 = jnp.where(first, own[0], oth[0]), jnp.where(first, own[2], oth[2])
         s1, c1, h1 = (jnp.where(first, oth[n], own[n]) for n in range(3))
-        through = dot(s0.astype(BF), c1.astype(BF), 1, 0)
-        out_ref[0][j] = jnp.where(keep, s0 + s1, s1).astype(BF)
-        out_ref[1][j] = jnp.where(keep, h0 + h1 + through, h1).astype(BF)
+        through = dot(c1.astype(BF), s0.astype(BF), 1, 1)
+        out_ref[0, j] = jnp.where(keep, s0 + s1, s1).astype(BF)
+        out_ref[1, j] = jnp.where(keep, h0 + h1 + through, h1).astype(BF)
 
 
 def output_kernel(blocks, heads, half, resets, q_ref, v_ref, w_ref, gain_ref, *refs):
-    same_ref, swap_ref, other_refs, out_ref = refs[:2], refs[2:4], refs[4:-1], refs[-1]
+    same_ref, swap_ref, other_refs, out_ref = refs[0], refs[1], refs[2:-1], refs[-1]
     step = heads // len(other_refs)
     length = q_ref.shape[0]
     _, core, chip, has, cut, has_second = scalars(resets, blocks, length)
@@ -107,18 +118,18 @@
         at = slice(h * HD, (h + 1) * HD)
         place = h % half
         mine = core == h // half
-        s_chip = jnp.where(mine, same_ref[0][place], swap_ref[0][place]).astype(F32)
-        h_chip = jnp.where(mine, same_ref[1][place], swap_ref[1][place]).astype(F32)
+        s_chip = jnp.where(mine, same_ref[0, place], swap_ref[0, place]).astype(F32)
+        h_chip = jnp.where(mine, same_ref[1, place], swap_ref[1, place]).astype(F32)
         s_chip = jnp.where(keep_chip, s_chip, 0.0)
         h_chip = jnp.where(keep_chip, h_chip, 0.0)
         s_in, c_in, h_in = (other_refs[h // step][n, h % step].astype(F32) for n in range(3))
-        through = dot(s_chip.astype(BF), c_in.astype(BF), 1, 0)
+        through = dot(c_in.astype(BF), s_chip.astype(BF), 1, 1)
         s_prev = jnp.where(second, s_chip + s_in, s_chip).astype(BF)
         h_prev = jnp.where(second, h_chip + h_in + through, h_chip).astype(BF)
         q, v = q_ref[:, at], v_ref[:, at]
         w = w_ref[:, at].astype(F32) + jnp.where(is_open, dot(q, s_prev, 1, 0), 0.0)
         scores = jnp.where(visible, dot(q, w.astype(BF), 1, 1), 0.0).astype(BF)
-        summed = dot(scores, v, 1, 0) + jnp.where(is_open, dot(q, h_prev, 1, 0), 0.0)
+        summed = dot(scores, v, 1, 0) + jnp.where(is_open, dot(q, h_prev, 1, 1), 0.0)
         inverse = lax.rsqrt(jnp.mean(summed * summed, axis=1, keepdims=True) + EPS)
         out_ref[:, at] = (summed * inverse * gain_ref[:, at]).astype(BF)
 
@@ -126,7 +137,7 @@
 def project_kernel(masks, hidden_ref, *refs):
     pairs = len(masks)
     same, other, (out_hbm, buffer, sems) = refs[:pairs], refs[pairs : 2 * pairs], refs[-3:]
-    index = lax.axis_index("ctx")
+    index, group = lax.axis_index("ctx"), lax.axis_index("groups")
     first = lax.rem(index, 2) == 0
     cols = 2 * same[0].shape[1]
     copies = []
@@ -134,7 +145,8 @@
         a, b = same[n][...], other[n][...]
         both = jnp.concatenate([jnp.where(first, a, b), jnp.where(first, b, a)], axis=1)
         buffer[n] = dot(hidden_ref[...], both, 1, 0).astype(BF)
-        at = pl.multiple_of(lax.div(index ^ mask, 2) * cols, cols)
+        place = index ^ jnp.where(group == 0, mask[0], mask[1])
+        at = pl.multiple_of(lax.div(place, 2) * cols, cols)
         copy = pltpu.make_async_copy(buffer.at[n], out_hbm.at[:, pl.ds(at, cols)], sems.at[n])
         copy.start()
         copies.append(copy)
@@ -170,22 +182,32 @@
     return [(i, i ^ mask) for i in range(n)]
 
 
-def on_device(blocks, queries, keys, values, reset_points, norm_gain, out_weight):
+def on_device(groups, blocks, queries, keys, values, reset_points, norm_gain, out_weight):
     length, width = queries.shape
     heads = width // HD
     half = heads // 2
     n_ctx = blocks
     per_span = n_ctx // reset_points.shape[0]
     assert per_span == 2 and heads % 2 == 0
-    small = n_ctx == 16 and out_weight.shape[1] == HD
-
-    def swap(piece, mask, *after):
-        if after:
-            piece, *_ = lax.optimization_barrier((piece, *after))
-        return lax.ppermute(piece, "ctx", swap_by(mask, n_ctx))
-
-    if small:
-        pieces = {0: out_weight, 2: swap(out_weight, 2), 4: swap(out_weight, 4), 8: swap(out_weight, 8)}
+    small = n_ctx == 16 and groups == 2 and out_weight.shape[1] == HD
+
+    def after(piece, *done):
+        return lax.optimization_barrier((piece, *done))[0] if done else piece
+
+    def swap(piece, mask, *done):
+        return lax.ppermute(after(piece, *done), "ctx", swap_by(mask, n_ctx))
+
+    def swap_groups(piece, *done):
+        return lax.ppermute(after(piece, *done), "groups", [(0, 1), (1, 0)])
+
+    if small:
+        far = [(g * n_ctx + i, g * n_ctx + (i ^ mask)) for g, mask in enumerate((8, 12)) for i in range(n_ctx)]
+        pieces = {
+            (0, 0): out_weight,
+            (2, 2): swap(out_weight, 2),
+            (4, 4): swap(out_weight, 4),
+            (8, 12): lax.ppermute(out_weight, ("groups", "ctx"), far),
+        }
 
     step_heads = 2
     steps = heads // step_heads
@@ -202,45 +224,44 @@
         name="block_state",
     )(reset_points, *(pltpu.with_memory_space_constraint(a, pltpu.HBM) for a in (queries, keys, values)))
     if small:
-        *state_sent, _, _ = lax.optimization_barrier((*state, pieces[2], pieces[4]))
+        *state_sent, _, _ = lax.optimization_barrier((*state, pieces[2, 2], pieces[4, 4]))
     else:
         state_sent = state
     state_other = [swap(part, 1) for part in state_sent]
-    waited = []
-    if small:
-        pieces[6] = swap(pieces[4], 2, w)
-        waited = [pieces[6], pieces[8]]
+    if small:
+        pieces[6, 6] = swap(pieces[4, 4], 2, w)
+    waited = [pieces[8, 12], pieces[6, 6]] if small else []
     chip_state = pl.pallas_call(
         functools.partial(chip_kernel, n_ctx, length, half, step_heads),
         in_specs=[smem()] + [whole_vmem] * (2 * steps) + [any_place] * len(waited),
-        out_shape=[jax.ShapeDtypeStruct((half, HD, HD), BF)] * 2,
+        out_shape=jax.ShapeDtypeStruct((2, half, HD, HD), BF),
         compiler_params=params(),
         name="chip_state",
     )(reset_points, *state, *state_other, *waited)
-    before = [lax.ppermute(part, "ctx", [(i, i + 2) for i in range(n_ctx - 2)]) for part in chip_state]
-    if small:
-        pieces[12] = swap(out_weight, 12, pieces[4])
-        for m in (8, 12):
-            pieces[m + 2] = swap(pieces[m], 2)
-        others = {m: swap(pieces[m], 1) for m in (0, 2, 4, 6, 8, 10, 12)}
-        before_swap = [swap(part, 1, pieces[12], pieces[10]) for part in before]
+    before = lax.ppermute(chip_state, "ctx", [(i, i + 2) for i in range(n_ctx - 2)])
+    if small:
+        pieces[10, 14] = swap(pieces[8, 12], 2)
+        pieces[12, 8] = swap_groups(pieces[8, 12])
+        pieces[14, 10] = swap_groups(pieces[10, 14])
+        others = {m: swap(pieces[m], 1) for m in pieces if m != (14, 10)}
+        before_swap = swap(before, 1, pieces[12, 8], pieces[10, 14])
     else:
-        before_swap = [swap(part, 1) for part in before]
+        before_swap = swap(before, 1)
     hidden = pl.pallas_call(
         functools.partial(output_kernel, n_ctx, heads, half),
-        in_specs=[smem()] + [whole_vmem] * (8 + steps),
+        in_specs=[smem()] + [whole_vmem] * (6 + steps),
         out_shape=jax.ShapeDtypeStruct((length, width), BF),
         compiler_params=params(),
         name="block_output",
-    )(reset_points, queries, values, w, norm_gain.reshape(1, width), *before, *before_swap, *state_other)
+    )(reset_points, queries, values, w, norm_gain.reshape(1, width), before, before_swap, *state_other)
     if not small:
         whole = lax.all_gather(out_weight, "ctx", axis=1, tiled=True)
         return jnp.dot(hidden, whole, preferred_element_type=F32).astype(BF)
     shape = jax.ShapeDtypeStruct((length, n_ctx * out_weight.shape[1]), BF)
-    masks = (0, 2, 4, 6, 8, 10, 12)
+    masks = tuple(others)
     out = project(hidden, masks, [pieces[m] for m in masks], [others[m] for m in masks], shape)
-    last = swap(pieces[14], 1, out)
-    return project(hidden, (14,), [pieces[14]], [last], shape, out)
+    last = swap(pieces[14, 10], 1, out)
+    return project(hidden, ((14, 10),), [pieces[14, 10]], [last], shape, out)
 
 
 def solution(mesh):
@@ -253,7 +274,7 @@
         P(None, "ctx"),
     )
     return jax.shard_map(
-        functools.partial(on_device, mesh.shape["ctx"]),
+        functools.partial(on_device, mesh.shape["groups"], mesh.shape["ctx"]),
         mesh=mesh,
         in_specs=placed,
         out_specs=P(("groups", "ctx"), None),

time: 48.2 us -> 45 us (0.934)
  the two profiles are of different devices: /device:TPU:13 before, /device:TPU:27 now
where the time goes in v3:
time: 45 us; the launch traced here: 44.1 us
  starting transfers between devices  20.3 us (45%)
  Pallas kernels  13.5 us (30%)
  waiting for transfers between devices  9.57 us (21%)
  local copies, waits for them, and re-layouts  0.68 us (2%)
    ppermute x17, starting transfers between devices, swap(): return lax.ppermute(after(piece, *done), 'ctx', swap_by(mask, n_ctx))  15.6 us
    ppermute x17, waiting for transfers between devices, swap(): return lax.ppermute(after(piece, *done), 'ctx', swap_by(mask, n_ctx))  7.32 us
    pallas_call x1, Pallas kernels, on_device(): pl.pallas_call(functools.partial(state_kernel, n_ctx, heads, step_heads),...  5.07 us
    pallas_call x1, Pallas kernels, on_device(): pl.pallas_call(functools.partial(output_kernel, n_ctx, heads, half), in_s...  4.06 us
    pallas_call x2, Pallas kernels, project(): pl.pallas_call(functools.partial(project_kernel, masks), in_specs=[pl.Blo...  3.55 us
    ppermute x2, starting transfers between devices, swap_groups(): return lax.ppermute(after(piece, *done), 'groups', [(0, 1), (1, 0)])  3.41 us
    ppermute x1, waiting for transfers between devices, on_device(): lax.ppermute(chip_state, 'ctx', [(i, i + 2) for i in range(n_ctx - 2)])  2.24 us
    ppermute x1, starting transfers between devices, on_device(): lax.ppermute(chip_state, 'ctx', [(i, i + 2) for i in range(n_ctx - 2)])  1.29 us
  transfers between devices with their start and end apart: 21, of which 5 were waited for; matrix products, arithmetic and copies ran while one was open for 0% of the time, Pallas kernels for 28%

profile of v3, /device:TPU:27, one launch (start us, length us, event | category | flops | bytes accessed | tf_op | source)
XLA Modules:
  0.0 44.1 jit_solution(7247026282393480738)
XLA Ops:
  0.0 0.2 collective-permute-start.1
  0.2 0.3 collective-permute-start
  0.4 0.7 %copy-done.3 = s32[8]{0:T(128)S(1)} copy-done((s32[8]{0:T(128)S(1)}, s32[8]{0:T(128)}, u32[]{:S(2)}) %copy-start.3) | copy-done | bytes 56
  1.1 5.1 %block_state.1 = (bf16[384,1024]{1,0:T(8,128)(2,1)S(1)}, bf16[3,2,128,128]{3,2,1,0:T(8,128)(2,1)S(1)}, bf16[3,2,128,128]{3,2,1,0:T(8,128)(2,1)S(1)}, bf16[3,2,12...) custom-call(s32[8]{0:T(128)S(1)} %copy-done.3, bf16[384,1024]{1,0:T(8,128)(2,1)} %q_ref.1, bf16[384,1024]{1,0:T(8,128)(2,1)} %k_hbm.1, ...), custom_call_target="tpu_custom_call" | custom-call | tf_op jit(solution)/shard_map/block_state/pallas_call | solution.py:216
  6.2 0.0 copy-start.2
  6.2 0.0 copy-start
  6.2 0.0 copy-start.1
  6.2 5.3 %collective-permute-done.1.refs_2_ = bf16[1024,128]{1,0:T(8,128)(2,1)S(1)} collective-permute-done((bf16[1024,128]{1,0:T(8,128)(2,1)}, bf16[1024,128]{1,0:T(8,128)(2,1)S(1)}, u32[]{:S(2)}, u32[]{:S(2)}) %collective-permute-start.1) | collective-permute-done | bytes 262176 | tf_op jit(solution)/shard_map/ppermute | solution.py:198
  11.5 1.5 %collective-permute-start.2 = (bf16[3,2,128,128]{3,2,1,0:T(8,128)(2,1)S(1)}, bf16[3,2,128,128]{3,2,1,0:T(8,128)(2,1)S(1)}, u32[]{:S(2)}, u32[]{:S(2)}) collective-permute-start(bf16[3,2,128,128]{3,2,1,0:T(8,128)(2,1)S(1)} %get-tuple-element.22.refs_0_), channel_id=1, source_target_pairs={{0,1},{1,0},{2,3},{3,2},{4,5},{5,4},{6,7},{7,6},{8,9},{9,8},{10,11... | collective-permute-start | bytes 589832 | tf_op jit(solution)/shard_map/ppermute | solution.py:198
  13.1 0.1 collective-permute-start.3
  13.1 0.4 collective-permute-start.4
  13.6 2.3 %collective-permute-start.5 = (bf16[3,2,128,128]{3,2,1,0:T(8,128)(2,1)S(1)}, bf16[3,2,128,128]{3,2,1,0:T(8,128)(2,1)S(1)}, u32[]{:S(2)}, u32[]{:S(2)}) collective-permute-start(bf16[3,2,128,128]{3,2,1,0:T(8,128)(2,1)S(1)} %get-tuple-element.25.refs_3_), channel_id=1, source_target_pairs={{0,1},{1,0},{2,3},{3,2},{4,5},{5,4},{6,7},{7,6},{8,9},{9,8},{10,11... | collective-permute-start | bytes 589832 | tf_op jit(solution)/shard_map/ppermute | solution.py:198
  15.9 1.2 %collective-permute-start.10 = (bf16[1024,128]{1,0:T(8,128)(2,1)S(1)}, bf16[1024,128]{1,0:T(8,128)(2,1)S(1)}, u32[]{:S(2)}, u32[]{:S(2)}) collective-permute-start(bf16[1024,128]{1,0:T(8,128)(2,1)S(1)} %collective-permute-done.6.refs_8_.refs_3_), channel_id=1, source_target_pairs={{0,2},{1,3},{2,0},{3,1},{4,6},{5,7},{6,4},{7,5},{8,10},{9,11},{10,... | collective-permute-start | bytes 786440 | tf_op jit(solution)/shard_map/ppermute | solution.py:198
  17.1 1.5 %collective-permute-start.9 = (bf16[1024,128]{1,0:T(8,128)(2,1)S(1)}, bf16[1024,128]{1,0:T(8,128)(2,1)S(1)}, u32[]{:S(2)}, u32[]{:S(2)}) collective-permute-start(bf16[1024,128]{1,0:T(8,128)(2,1)S(1)} %collective-permute-done.6.refs_8_.refs_3_), channel_id=1, source_target_pairs={{0,16},{16,0},{1,17},{17,1},{2,18},{18,2},{3,19},{19,3},{4,20},{20... | collective-permute-start | bytes 786440 | tf_op jit(solution)/shard_map/ppermute | solution.py:201
  18.6 0.8 %chip_state.1 = bf16[2,4,128,128]{3,2,1,0:T(8,128)(2,1)S(1)} custom-call(s32[8]{0:T(128)S(1)} %copy-done.3, bf16[3,2,128,128]{3,2,1,0:T(8,128)(2,1)S(1)} %get-tuple-element.22.refs_0_, bf16[3,2,128,128]{3,2,1,0:T(8,128)(2,1)S(1)} %get-tuple-element.23.refs_1_, bf16[3,2,128,128]{3,2,1,0:T(8,128)(2,1)S(1)} %get-tuple-element.24.refs_2_, ...), custom_call_target="tpu_custom_call" | custom-call | tf_op jit(solution)/shard_map/chip_state/pallas_call | solution.py:234
  19.4 1.3 %collective-permute-start.8 = (bf16[2,4,128,128]{3,2,1,0:T(8,128)(2,1)S(1)}, bf16[2,4,128,128]{3,2,1,0:T(8,128)(2,1)S(1)}, u32[]{:S(2)}, u32[]{:S(2)}) collective-permute-start(bf16[2,4,128,128]{3,2,1,0:T(8,128)(2,1)S(1)} %chip_state.1), channel_id=1, source_target_pairs={{0,2},{1,3},{2,4},{3,5},{4,6},{5,7},{6,8},{7,9},{8,10},{9,11},{10,... | collective-permute-start | bytes 786440 | tf_op jit(solution)/shard_map/ppermute | solution.py:241
  20.8 2.8 %collective-permute-start.13 = (bf16[1024,128]{1,0:T(8,128)(2,1)S(1)}, bf16[1024,128]{1,0:T(8,128)(2,1)S(1)}, u32[]{:S(2)}, u32[]{:S(2)}) collective-permute-start(bf16[1024,128]{1,0:T(8,128)(2,1)S(1)} %copy-done.2), channel_id=1, source_target_pairs={{0,1},{1,0},{2,3},{3,2},{4,5},{5,4},{6,7},{7,6},{8,9},{9,8},{10,11... | collective-permute-start | bytes 786440 | tf_op jit(solution)/shard_map/ppermute | solution.py:198
  23.5 0.1 collective-permute-start.16
  23.6 0.7 %collective-permute-done.10.refs_5_ = bf16[1024,128]{1,0:T(8,128)(2,1)S(1)} collective-permute-done((bf16[1024,128]{1,0:T(8,128)(2,1)S(1)}, bf16[1024,128]{1,0:T(8,128)(2,1)S(1)}, u32[]{:S(2)}, u32[]{:S(2)}) %collective-permute-start.10) | collective-permute-done | bytes 262176 | tf_op jit(solution)/shard_map/ppermute | solution.py:198
  24.3 2.7 %collective-permute-start.15 = (bf16[1024,128]{1,0:T(8,128)(2,1)S(1)}, bf16[1024,128]{1,0:T(8,128)(2,1)S(1)}, u32[]{:S(2)}, u32[]{:S(2)}) collective-permute-start(bf16[1024,128]{1,0:T(8,128)(2,1)S(1)} %collective-permute-done.1.refs_2_), channel_id=1, source_target_pairs={{0,1},{1,0},{2,3},{3,2},{4,5},{5,4},{6,7},{7,6},{8,9},{9,8},{10,11... | collective-permute-start | bytes 786440 | tf_op jit(solution)/shard_map/ppermute | solution.py:198
  27.0 2.2 %collective-permute-done.8.refs_0_ = bf16[2,4,128,128]{3,2,1,0:T(8,128)(2,1)S(1)} collective-permute-done((bf16[2,4,128,128]{3,2,1,0:T(8,128)(2,1)S(1)}, bf16[2,4,128,128]{3,2,1,0:T(8,128)(2,1)S(1)}, u32[]{:S(2)}, u32[]{:S(2)}) %collective-permute-start.8) | collective-permute-done | bytes 262176 | tf_op jit(solution)/shard_map/ppermute | solution.py:241
  29.2 2.2 %collective-permute-start.11 = (bf16[2,4,128,128]{3,2,1,0:T(8,128)(2,1)S(1)}, bf16[2,4,128,128]{3,2,1,0:T(8,128)(2,1)S(1)}, u32[]{:S(2)}, u32[]{:S(2)}) collective-permute-start(bf16[2,4,128,128]{3,2,1,0:T(8,128)(2,1)S(1)} %collective-permute-done.8.refs_0_), channel_id=1, source_target_pairs={{0,1},{1,0},{2,3},{3,2},{4,5},{5,4},{6,7},{7,6},{8,9},{9,8},{10,11... | collective-permute-start | bytes 786440 | tf_op jit(solution)/shard_map/ppermute | solution.py:198
  31.5 0.5 %collective-permute-start.17 = (bf16[1024,128]{1,0:T(8,128)(2,1)S(1)}, bf16[1024,128]{1,0:T(8,128)(2,1)S(1)}, u32[]{:S(2)}, u32[]{:S(2)}) collective-permute-start(bf16[1024,128]{1,0:T(8,128)(2,1)S(1)} %collective-permute-done.7.refs_9_.refs_4_), channel_id=1, source_target_pairs={{0,1},{1,0},{2,3},{3,2},{4,5},{5,4},{6,7},{7,6},{8,9},{9,8},{10,11... | collective-permute-start | bytes 786440 | tf_op jit(solution)/shard_map/ppermute | solution.py:198
  32.0 0.1 collective-permute-start.18
  32.1 0.4 collective-permute-start.19
  32.5 0.1 collective-permute-done.11.refs_1_
  32.6 1.9 %collective-permute-start.12 = (bf16[1024,128]{1,0:T(8,128)(2,1)S(1)}, bf16[1024,128]{1,0:T(8,128)(2,1)S(1)}, u32[]{:S(2)}, u32[]{:S(2)}) collective-permute-start(bf16[1024,128]{1,0:T(8,128)(2,1)S(1)} %collective-permute-done.10.refs_5_), channel_id=1, source_target_pairs={{0,16},{16,0},{1,17},{17,1},{2,18},{18,2},{3,19},{19,3},{4,20},{20... | collective-permute-start | bytes 786440 | tf_op jit(solution)/shard_map/ppermute | solution.py:201
  34.6 4.1 %block_output.1.hidden_ref = bf16[384,1024]{1,0:T(8,128)(2,1)S(1)} custom-call(s32[8]{0:T(128)S(1)} %copy-done.3, bf16[384,1024]{1,0:T(8,128)(2,1)S(1)} %copy-done, bf16[384,1024]{1,0:T(8,128)(2,1)S(1)} %copy-done.1, bf16[384,1024]{1,0:T(8,128)(2,1)S(1)} %get-tuple-element.17.w_ref, f32[1,1024]{1,0:T(1,128)S(1)} %bitcast.1, ...), custom_call_target="tpu_custom_call" | custom-call | tf_op jit(solution)/shard_map/block_output/pallas_call | solution.py:250
  38.7 2.5 %project.2.refs_2_ = bf16[384,2048]{1,0:T(8,128)(2,1)} custom-call(bf16[384,1024]{1,0:T(8,128)(2,1)S(1)} %block_output.1.hidden_ref, bf16[1024,128]{1,0:T(8,128)(2,1)S(1)} %copy-done.2, bf16[1024,128]{1,0:T(8,128)(2,1)S(1)} %collective-permute-done.refs_1_, bf16[1024,128]{1,0:T(8,128)(2,1)S(1)} %collective-permute-done.1.refs_2_, ...), custom_call_target="tpu_custom_call" | custom-call | tf_op jit(solution)/shard_map/project/pallas_call | solution.py:161
  41.2 0.7 %collective-permute-start.20 = (bf16[1024,128]{1,0:T(8,128)(2,1)S(1)}, bf16[1024,128]{1,0:T(8,128)(2,1)S(1)}, u32[]{:S(2)}, u32[]{:S(2)}) collective-permute-start(bf16[1024,128]{1,0:T(8,128)(2,1)S(1)} %collective-permute-done.12.refs_0_), channel_id=1, source_target_pairs={{0,1},{1,0},{2,3},{3,2},{4,5},{5,4},{6,7},{7,6},{8,9},{9,8},{10,11... | collective-permute-start | bytes 786440 | tf_op jit(solution)/shard_map/ppermute | solution.py:198
  41.9 1.2 %collective-permute-done.20.refs_1_ = bf16[1024,128]{1,0:T(8,128)(2,1)S(1)} collective-permute-done((bf16[1024,128]{1,0:T(8,128)(2,1)S(1)}, bf16[1024,128]{1,0:T(8,128)(2,1)S(1)}, u32[]{:S(2)}, u32[]{:S(2)}) %collective-permute-start.20) | collective-permute-done | bytes 262176 | tf_op jit(solution)/shard_map/ppermute | solution.py:198
  43.1 1.1 %project.3 = bf16[384,2048]{1,0:T(8,128)(2,1)} custom-call(bf16[384,1024]{1,0:T(8,128)(2,1)S(1)} %block_output.1.hidden_ref, bf16[1024,128]{1,0:T(8,128)(2,1)S(1)} %collective-permute-done.12.refs_0_, bf16[1024,128]{1,0:T(8,128)(2,1)S(1)} %collective-permute-done.20.refs_1_, bf16[384,2048]{1,0:T(8,128)(2,1)} %project.2.refs_2_), custom_call_target="tpu_custom_call", output_to_operand_aliasing={{}: (3, {})} | custom-call | tf_op jit(solution)/shard_map/project/pallas_call | solution.py:161
  (25 shorter events, 0.1 us)
Async XLA Ops:
  0.0 11.5 %collective-permute-start.1 = (bf16[1024,128]{1,0:T(8,128)(2,1)}, bf16[1024,128]{1,0:T(8,128)(2,1)S(1)}, u32[]{:S(2)}, u32[]{:S(2)}) collective-permute-start(bf16[1024,128]{1,0:T(8,128)(2,1)} %refs_0_.1), channel_id=1, source_target_pairs={{0,4},{1,5},{2,6},{3,7},{4,0},{5,1},{6,2},{7,3},{8,12},{9,13},{10,... | collective-permute-start | bytes 786440 | tf_op jit(solution)/shard_map/ppermute | solution.py:198
  0.2 11.3 %collective-permute-start = (bf16[1024,128]{1,0:T(8,128)(2,1)}, bf16[1024,128]{1,0:T(8,128)(2,1)S(1)}, u32[]{:S(2)}, u32[]{:S(2)}) collective-permute-start(bf16[1024,128]{1,0:T(8,128)(2,1)} %refs_0_.1), channel_id=1, source_target_pairs={{0,2},{1,3},{2,0},{3,1},{4,6},{5,7},{6,4},{7,5},{8,10},{9,11},{10,... | collective-permute-start | bytes 786440 | tf_op jit(solution)/shard_map/ppermute | solution.py:198
  0.4 13.1 %collective-permute-start.6 = (bf16[1024,128]{1,0:T(8,128)(2,1)}, bf16[1024,128]{1,0:T(8,128)(2,1)S(1)}, u32[]{:S(2)}, u32[]{:S(2)}) collective-permute-start(bf16[1024,128]{1,0:T(8,128)(2,1)} %refs_0_.1), channel_id=1, source_target_pairs={{0,8},{1,9},{2,10},{3,11},{4,12},{5,13},{6,14},{7,15},{8,0},{9,1},... | collective-permute-start | bytes 786440 | tf_op jit(solution)/shard_map/ppermute | solution.py:209
  0.4 0.7 %copy-start.3 = (s32[8]{0:T(128)S(1)}, s32[8]{0:T(128)}, u32[]{:S(2)}) copy-start(s32[8]{0:T(128)} %resets.5) | copy-start | bytes 100
  6.2 14.6 %copy-start.2 = (bf16[1024,128]{1,0:T(8,128)(2,1)S(1)}, bf16[1024,128]{1,0:T(8,128)(2,1)}, u32[]{:S(2)}) copy-start(bf16[1024,128]{1,0:T(8,128)(2,1)} %refs_0_.1) | copy-start | bytes 786436
  6.2 28.4 %copy-start = (bf16[384,1024]{1,0:T(8,128)(2,1)S(1)}, bf16[384,1024]{1,0:T(8,128)(2,1)}, u32[]{:S(2)}) copy-start(bf16[384,1024]{1,0:T(8,128)(2,1)} %q_ref.1) | copy-start | bytes 2359300
  6.2 28.4 %copy-start.1 = (bf16[384,1024]{1,0:T(8,128)(2,1)S(1)}, bf16[384,1024]{1,0:T(8,128)(2,1)}, u32[]{:S(2)}) copy-start(bf16[384,1024]{1,0:T(8,128)(2,1)} %v_ref.1) | copy-start | bytes 2359300
  6.2 28.4 %copy-start.4 = (f32[1024]{0:T(1024)S(1)}, f32[1024]{0:T(1024)}, u32[]{:S(2)}) copy-start(f32[1024]{0:T(1024)} %param.10) | copy-start | bytes 12292
  11.5 7.1 %collective-permute-start.7 = (bf16[1024,128]{1,0:T(8,128)(2,1)S(1)}, bf16[1024,128]{1,0:T(8,128)(2,1)S(1)}, u32[]{:S(2)}, u32[]{:S(2)}) collective-permute-start(bf16[1024,128]{1,0:T(8,128)(2,1)S(1)} %collective-permute-done.1.refs_2_), channel_id=1, source_target_pairs={{0,2},{1,3},{2,0},{3,1},{4,6},{5,7},{6,4},{7,5},{8,10},{9,11},{10,... | collective-permute-start | bytes 786440 | tf_op jit(solution)/shard_map/ppermute | solution.py:198
  11.5 4.4 %collective-permute-start.2 = (bf16[3,2,128,128]{3,2,1,0:T(8,128)(2,1)S(1)}, bf16[3,2,128,128]{3,2,1,0:T(8,128)(2,1)S(1)}, u32[]{:S(2)}, u32[]{:S(2)}) collective-permute-start(bf16[3,2,128,128]{3,2,1,0:T(8,128)(2,1)S(1)} %get-tuple-element.22.refs_0_), channel_id=1, source_target_pairs={{0,1},{1,0},{2,3},{3,2},{4,5},{5,4},{6,7},{7,6},{8,9},{9,8},{10,11... | collective-permute-start | bytes 589832 | tf_op jit(solution)/shard_map/ppermute | solution.py:198
  13.1 4.1 %collective-permute-start.3 = (bf16[3,2,128,128]{3,2,1,0:T(8,128)(2,1)S(1)}, bf16[3,2,128,128]{3,2,1,0:T(8,128)(2,1)S(1)}, u32[]{:S(2)}, u32[]{:S(2)}) collective-permute-start(bf16[3,2,128,128]{3,2,1,0:T(8,128)(2,1)S(1)} %get-tuple-element.23.refs_1_), channel_id=1, source_target_pairs={{0,1},{1,0},{2,3},{3,2},{4,5},{5,4},{6,7},{7,6},{8,9},{9,8},{10,11... | collective-permute-start | bytes 589832 | tf_op jit(solution)/shard_map/ppermute | solution.py:198
  13.1 5.5 %collective-permute-start.4 = (bf16[3,2,128,128]{3,2,1,0:T(8,128)(2,1)S(1)}, bf16[3,2,128,128]{3,2,1,0:T(8,128)(2,1)S(1)}, u32[]{:S(2)}, u32[]{:S(2)}) collective-permute-start(bf16[3,2,128,128]{3,2,1,0:T(8,128)(2,1)S(1)} %get-tuple-element.24.refs_2_), channel_id=1, source_target_pairs={{0,1},{1,0},{2,3},{3,2},{4,5},{5,4},{6,7},{7,6},{8,9},{9,8},{10,11... | collective-permute-start | bytes 589832 | tf_op jit(solution)/shard_map/ppermute | solution.py:198
  13.6 5.0 %collective-permute-start.5 = (bf16[3,2,128,128]{3,2,1,0:T(8,128)(2,1)S(1)}, bf16[3,2,128,128]{3,2,1,0:T(8,128)(2,1)S(1)}, u32[]{:S(2)}, u32[]{:S(2)}) collective-permute-start(bf16[3,2,128,128]{3,2,1,0:T(8,128)(2,1)S(1)} %get-tuple-element.25.refs_3_), channel_id=1, source_target_pairs={{0,1},{1,0},{2,3},{3,2},{4,5},{5,4},{6,7},{7,6},{8,9},{9,8},{10,11... | collective-permute-start | bytes 589832 | tf_op jit(solution)/shard_map/ppermute | solution.py:198
  15.9 8.4 %collective-permute-start.10 = (bf16[1024,128]{1,0:T(8,128)(2,1)S(1)}, bf16[1024,128]{1,0:T(8,128)(2,1)S(1)}, u32[]{:S(2)}, u32[]{:S(2)}) collective-permute-start(bf16[1024,128]{1,0:T(8,128)(2,1)S(1)} %collective-permute-done.6.refs_8_.refs_3_), channel_id=1, source_target_pairs={{0,2},{1,3},{2,0},{3,1},{4,6},{5,7},{6,4},{7,5},{8,10},{9,11},{10,... | collective-permute-start | bytes 786440 | tf_op jit(solution)/shard_map/ppermute | solution.py:198
  17.1 9.8 %collective-permute-start.9 = (bf16[1024,128]{1,0:T(8,128)(2,1)S(1)}, bf16[1024,128]{1,0:T(8,128)(2,1)S(1)}, u32[]{:S(2)}, u32[]{:S(2)}) collective-permute-start(bf16[1024,128]{1,0:T(8,128)(2,1)S(1)} %collective-permute-done.6.refs_8_.refs_3_), channel_id=1, source_target_pairs={{0,16},{16,0},{1,17},{17,1},{2,18},{18,2},{3,19},{19,3},{4,20},{20... | collective-permute-start | bytes 786440 | tf_op jit(solution)/shard_map/ppermute | solution.py:201
  19.4 9.8 %collective-permute-start.8 = (bf16[2,4,128,128]{3,2,1,0:T(8,128)(2,1)S(1)}, bf16[2,4,128,128]{3,2,1,0:T(8,128)(2,1)S(1)}, u32[]{:S(2)}, u32[]{:S(2)}) collective-permute-start(bf16[2,4,128,128]{3,2,1,0:T(8,128)(2,1)S(1)} %chip_state.1), channel_id=1, source_target_pairs={{0,2},{1,3},{2,4},{3,5},{4,6},{5,7},{6,8},{7,9},{8,10},{9,11},{10,... | collective-permute-start | bytes 786440 | tf_op jit(solution)/shard_map/ppermute | solution.py:241
  20.8 10.7 %collective-permute-start.13 = (bf16[1024,128]{1,0:T(8,128)(2,1)S(1)}, bf16[1024,128]{1,0:T(8,128)(2,1)S(1)}, u32[]{:S(2)}, u32[]{:S(2)}) collective-permute-start(bf16[1024,128]{1,0:T(8,128)(2,1)S(1)} %copy-done.2), channel_id=1, source_target_pairs={{0,1},{1,0},{2,3},{3,2},{4,5},{5,4},{6,7},{7,6},{8,9},{9,8},{10,11... | collective-permute-start | bytes 786440 | tf_op jit(solution)/shard_map/ppermute | solution.py:198
  23.5 8.4 %collective-permute-start.16 = (bf16[1024,128]{1,0:T(8,128)(2,1)S(1)}, bf16[1024,128]{1,0:T(8,128)(2,1)S(1)}, u32[]{:S(2)}, u32[]{:S(2)}) collective-permute-start(bf16[1024,128]{1,0:T(8,128)(2,1)S(1)} %collective-permute-done.6.refs_8_.refs_3_), channel_id=1, source_target_pairs={{0,1},{1,0},{2,3},{3,2},{4,5},{5,4},{6,7},{7,6},{8,9},{9,8},{10,11... | collective-permute-start | bytes 786440 | tf_op jit(solution)/shard_map/ppermute | solution.py:198
  24.3 7.7 %collective-permute-start.15 = (bf16[1024,128]{1,0:T(8,128)(2,1)S(1)}, bf16[1024,128]{1,0:T(8,128)(2,1)S(1)}, u32[]{:S(2)}, u32[]{:S(2)}) collective-permute-start(bf16[1024,128]{1,0:T(8,128)(2,1)S(1)} %collective-permute-done.1.refs_2_), channel_id=1, source_target_pairs={{0,1},{1,0},{2,3},{3,2},{4,5},{5,4},{6,7},{7,6},{8,9},{9,8},{10,11... | collective-permute-start | bytes 786440 | tf_op jit(solution)/shard_map/ppermute | solution.py:198
  29.2 3.4 %collective-permute-start.11 = (bf16[2,4,128,128]{3,2,1,0:T(8,128)(2,1)S(1)}, bf16[2,4,128,128]{3,2,1,0:T(8,128)(2,1)S(1)}, u32[]{:S(2)}, u32[]{:S(2)}) collective-permute-start(bf16[2,4,128,128]{3,2,1,0:T(8,128)(2,1)S(1)} %collective-permute-done.8.refs_0_), channel_id=1, source_target_pairs={{0,1},{1,0},{2,3},{3,2},{4,5},{5,4},{6,7},{7,6},{8,9},{9,8},{10,11... | collective-permute-start | bytes 786440 | tf_op jit(solution)/shard_map/ppermute | solution.py:198
  31.5 7.2 %collective-permute-start.14 = (bf16[1024,128]{1,0:T(8,128)(2,1)S(1)}, bf16[1024,128]{1,0:T(8,128)(2,1)S(1)}, u32[]{:S(2)}, u32[]{:S(2)}) collective-permute-start(bf16[1024,128]{1,0:T(8,128)(2,1)S(1)} %collective-permute-done.refs_1_), channel_id=1, source_target_pairs={{0,1},{1,0},{2,3},{3,2},{4,5},{5,4},{6,7},{7,6},{8,9},{9,8},{10,11... | collective-permute-start | bytes 786440 | tf_op jit(solution)/shard_map/ppermute | solution.py:198
  31.5 7.2 %collective-permute-start.17 = (bf16[1024,128]{1,0:T(8,128)(2,1)S(1)}, bf16[1024,128]{1,0:T(8,128)(2,1)S(1)}, u32[]{:S(2)}, u32[]{:S(2)}) collective-permute-start(bf16[1024,128]{1,0:T(8,128)(2,1)S(1)} %collective-permute-done.7.refs_9_.refs_4_), channel_id=1, source_target_pairs={{0,1},{1,0},{2,3},{3,2},{4,5},{5,4},{6,7},{7,6},{8,9},{9,8},{10,11... | collective-permute-start | bytes 786440 | tf_op jit(solution)/shard_map/ppermute | solution.py:198
  32.0 6.7 %collective-permute-start.18 = (bf16[1024,128]{1,0:T(8,128)(2,1)S(1)}, bf16[1024,128]{1,0:T(8,128)(2,1)S(1)}, u32[]{:S(2)}, u32[]{:S(2)}) collective-permute-start(bf16[1024,128]{1,0:T(8,128)(2,1)S(1)} %collective-permute-done.10.refs_5_), channel_id=1, source_target_pairs={{0,1},{1,0},{2,3},{3,2},{4,5},{5,4},{6,7},{7,6},{8,9},{9,8},{10,11... | collective-permute-start | bytes 786440 | tf_op jit(solution)/shard_map/ppermute | solution.py:198
  32.1 6.6 %collective-permute-start.19 = (bf16[1024,128]{1,0:T(8,128)(2,1)S(1)}, bf16[1024,128]{1,0:T(8,128)(2,1)S(1)}, u32[]{:S(2)}, u32[]{:S(2)}) collective-permute-start(bf16[1024,128]{1,0:T(8,128)(2,1)S(1)} %collective-permute-done.9.refs_6_), channel_id=1, source_target_pairs={{0,1},{1,0},{2,3},{3,2},{4,5},{5,4},{6,7},{7,6},{8,9},{9,8},{10,11... | collective-permute-start | bytes 786440 | tf_op jit(solution)/shard_map/ppermute | solution.py:198
  32.6 8.5 %collective-permute-start.12 = (bf16[1024,128]{1,0:T(8,128)(2,1)S(1)}, bf16[1024,128]{1,0:T(8,128)(2,1)S(1)}, u32[]{:S(2)}, u32[]{:S(2)}) collective-permute-start(bf16[1024,128]{1,0:T(8,128)(2,1)S(1)} %collective-permute-done.10.refs_5_), channel_id=1, source_target_pairs={{0,16},{16,0},{1,17},{17,1},{2,18},{18,2},{3,19},{19,3},{4,20},{20... | collective-permute-start | bytes 786440 | tf_op jit(solution)/shard_map/ppermute | solution.py:201
  41.2 1.9 %collective-permute-start.20 = (bf16[1024,128]{1,0:T(8,128)(2,1)S(1)}, bf16[1024,128]{1,0:T(8,128)(2,1)S(1)}, u32[]{:S(2)}, u32[]{:S(2)}) collective-permute-start(bf16[1024,128]{1,0:T(8,128)(2,1)S(1)} %collective-permute-done.12.refs_0_), channel_id=1, source_target_pairs={{0,1},{1,0},{2,3},{3,2},{4,5},{5,4},{6,7},{7,6},{8,9},{9,8},{10,11... | collective-permute-start | bytes 786440 | tf_op jit(solution)/shard_map/ppermute | solution.py:198
